TPU v7x, 256 devices: a whole 4x4x8 slice. The times are simulated.
256 devices in a mesh: dp: 64 (over z, y, core), seq: 4 (over x).
Axes of the slice: x: 4, y: 4, z: 8, core: 2. Of those that a mesh axis runs over, the one named last changes fastest.
Arguments:
- loader_frames: bfloat16 [4, 4096, 640], P('seq', 'dp'), may hold values from -6 to 6
- block_dest: int32 [4, 4096], P('seq'), may hold values from 0 to 4095, as said below
- utt_lengths: int32 [64, 3], P('dp'), may hold values from 1 to 128, 256 in all within a row
- conv1_weight: bfloat16 [9, 512], replicated, may hold values from -2 to 2
- conv2_weight: bfloat16 [9, 512, 512], replicated, may hold values from -0.09375 to 0.09375
- proj_weight: bfloat16 [9728, 768], P('dp')
- gain_in: float32 [768], replicated, may hold values from 0.5 to 2
- point_in: bfloat16 [768, 1536], replicated, may hold values from -0.21875 to 0.21875
- taps: float32 [31, 768], replicated, may hold values from -1 to 1
- gain_mid: float32 [768], replicated, may hold values from 0.5 to 2
- point_out: bfloat16 [768, 768], replicated, may hold values from -0.21875 to 0.21875
- grad_encoded: bfloat16 [64, 512, 768], P('dp', 'seq'), may hold values from -6 to 6
Outputs:
- encoded: bfloat16 [64, 512, 768], P('dp', 'seq')
- grad_input: bfloat16 [64, 512, 768], P('dp', 'seq')
Inputs may be any that keep to these rules, and one draw needn't show every extreme that they name: `block_dest`: for every seq index the row is a permutation. Of the 64 blocks at one dp index, at most 2 go to slots of one dp index (slot // 64), and every dp index sends exactly 2 to some dp index. `utt_lengths`: each row sums to 256; its longest utterance has exactly 128 blocks.
All inputs are finite; a program needn't handle non-finite values.
Results may differ from a plain program's by a relative error of at most 0.02.
Values may be sent and summed in bfloat16 or wider, within the bound.
No kernel may reach another device: no remote copies, remote signals or barrier semaphores. Data moves between devices by JAX's collectives and lax.ppermute only.
A program may use at most 128 MiB of HBM per device.

v0:
```python
import functools

import jax
import jax.numpy as jnp
import numpy as np
from jax import lax
from jax.experimental import pallas as pl
from jax.experimental.pallas import tpu as pltpu
from jax.sharding import PartitionSpec as P

BLK = 8
PITCH = 32
WIDE = BLK * PITCH
MEL_STEP = 20
MEL_LEAD = 4
MEL_KEEP = 27
FULL = 4
BINS = FULL + 1
BINS_IN = 13
BIN_ORDER = tuple(range(0, BINS_IN, 2)) + tuple(range(1, BINS_IN, 2))
EVENS = (BINS_IN + 1) // 2
RIM = 32
PROJ_PARTS = 4
CONV_ROWS = 256
F32 = jnp.float32
BF16 = jnp.bfloat16
VMEM = pl.BlockSpec(memory_space=pltpu.VMEM)
SMEM = pl.BlockSpec(memory_space=pltpu.SMEM)
HBM = pl.BlockSpec(memory_space=pltpu.HBM)


def iota(shape, dim):
    return lax.broadcasted_iota(jnp.int32, shape, dim)


def one_hot(condition):
    return jnp.where(condition, 1.0, 0.0).astype(BF16)


def dot(left, right):
    return jnp.dot(left, right, preferred_element_type=F32)


def dot_rows(left, right):
    return lax.dot_general(left, right, (((0,), (0,)), ((), ())), preferred_element_type=F32)


def dot_cols(left, right):
    return lax.dot_general(left, right, (((1,), (1,)), ((), ())), preferred_element_type=F32)


def send_kernel(place_ref, frames_ref, dest_ref, proj_ref, out_ref, same_ref, other_ref):
    group = place_ref[0]
    blocks = frames_ref.shape[0]
    span = pl.multiple_of((group // 2) * 128, 128)
    pair = dest_ref[:, pl.ds(span, 128)]
    pair = jnp.where(group % 2 == 1, pltpu.roll(pair, 128 - blocks, 1), pair)
    row = jnp.broadcast_to(pair, (128, 128)) // blocks
    at_row, at_col = iota((128, 128), 0), iota((128, 128), 1)
    column = jnp.sum(jnp.where(at_row == at_col, row, 0), axis=1, keepdims=True)
    same = (row == column) & (at_row < at_col) & (at_row < blocks)
    rank = jnp.sum(jnp.where(same, 1, 0), axis=0, keepdims=True)
    slot = (row[0:1] * 2 + rank)[:, 0:blocks]
    sorted_blocks = dot(one_hot(iota((2 * blocks, blocks), 0) == slot), frames_ref[...])
    out_ref[...] = sorted_blocks.astype(BF16).reshape(out_ref.shape)
    half = same_ref.shape[1]
    left, right = proj_ref[:, 0:half], proj_ref[:, half : 2 * half]
    odd = group % 2 == 1
    same_ref[...] = jnp.where(odd, right, left)
    other_ref[...] = jnp.where(odd, left, right)


def landing_kernel(place_ref, dest_ref, out_ref):
    group = place_ref[0]
    groups, blocks = dest_ref.shape
    dest = dest_ref[...]
    mine = dest // blocks == group
    earlier = one_hot(iota((blocks, blocks), 0) < iota((blocks, blocks), 1))
    rank = dot(one_hot(mine), earlier)
    spot = dest % blocks
    for copy in range(2):
        kept = jnp.where(mine & (rank == float(copy)), spot + 1, 0)
        landing = jnp.sum(kept, axis=1, keepdims=True) - 1
        out_ref[copy] = one_hot(iota((groups, blocks), 1) == landing)


def place_kernel(place_ref, arrived_ref, landing_ref, cut_ref, cot_ref, *out_refs):
    group, seat = place_ref[0], place_ref[1]
    window_ref = out_refs[-1]
    blocks = landing_ref.shape[2]
    arrived = arrived_ref[...]
    placed = dot_rows(landing_ref[0], arrived[:, 0, :]) + dot_rows(
        landing_ref[1], arrived[:, 1, :]
    )
    seats = len(out_refs) - 1
    window_ref[...] = dot(placed.astype(BF16), cut_ref[...]).astype(BF16)
    count = cot_ref.shape[0]
    for step in range(seats):
        share = ((seat + step) % seats) ^ (group // 16)
        span = pl.ds(pl.multiple_of(share * WIDE, WIDE), WIDE)
        out_refs[step][0:blocks, :] = window_ref[:, span]
        if step in (1, seats - 1):
            begin = count - 16 if step == 1 else 0
            for piece in range(cot_ref.shape[1] // WIDE):
                columns = slice(piece * WIDE, (piece + 1) * WIDE)
                rows = slice(blocks + 16 * piece, blocks + 16 * piece + 16)
                out_refs[step][rows, :] = cot_ref[begin : begin + 16, columns]


def row_starts(share):
    start_a = jnp.where(share == 0, 2176, jnp.where(share == 2, 128, 0))
    start_b = jnp.where(share == 1, 2304, jnp.where(share == 3, 256, 2432))
    return 128 * share + 128, start_a, start_b


def proj_copies(core, same_hbm, other_hbm, proj_ref, sems):
    rows, half = same_hbm.shape
    parts = sems.shape[0] // 2
    size = rows // parts

    def copy(here, part, side):
        source = same_hbm if here == side else other_hbm
        return pltpu.make_async_copy(
            source.at[pl.ds(part * size, size)],
            proj_ref.at[pl.ds(128 + part * size, size), pl.ds(side * half, half)],
            sems.at[2 * part + side],
        )

    def start():
        for here in range(2):

            @pl.when(core == here)
            def _():
                for part in range(parts):
                    for side in range(2):
                        copy(here, part, side).start()

    def wait(part):
        for side in range(2):
            copy(0, part, side).wait()

    return start, wait


def project(features, share, proj_ref, wait):
    start, start_a, start_b = row_starts(share)
    result = None
    wait(0)
    for index in range(FULL + 2):
        if index < PROJ_PARTS - 1:
            wait(index + 1)
        if index < FULL:
            at, size, column = start + 512 * index, 512, 512 * index
        else:
            at, size = (start_a, 256) if index == FULL else (start_b, 256)
            column = 512 * FULL + 256 * (index - FULL)
        weight = proj_ref[pl.ds(pl.multiple_of(at, 128), size), :]
        part = dot(features(column, size), weight)
        result = part if result is None else result + part
    return result


def zero_rims(proj_ref, rows):
    rim = jnp.zeros((128, proj_ref.shape[1]), BF16)
    proj_ref[0:128, :] = rim
    proj_ref[128 + rows : 256 + rows, :] = rim


def conv_kernel(place_ref, lengths_ref, *refs):
    block_refs, (conv1_ref, conv2_hbm), refs = refs[:4], refs[4:6], refs[6:]
    out_ref, conv2_ref, patch_ref, first_ref, conv2_sems = refs
    group, seat = place_ref[0], place_ref[1]
    share = seat ^ (group // 16)
    taps, channels = conv2_ref.shape[0], conv2_ref.shape[1]
    frames = out_ref.shape[0]
    conv2_copies = [
        pltpu.make_async_copy(conv2_hbm.at[tap], conv2_ref.at[tap], conv2_sems.at[tap])
        for tap in range(taps)
    ]
    for copy in conv2_copies:
        copy.start()
    windows = jnp.concatenate([block_ref[0:64, :] for block_ref in block_refs], axis=0)
    count = windows.shape[0]
    frame = (seat * 128 + iota((frames, count), 0)) % (2 * count)
    block = iota((frames, count), 1)
    block = ((seat + 4 - block // 64) % 4) * 64 + block % 64
    own_block = frame // 2
    second = lengths_ref[0]
    third = second + lengths_ref[1]
    begins = (own_block == 0) | (own_block == second) | (own_block == third)
    odd = frame % 2 == 1
    here = own_block == block
    before = (own_block - 1 == block) & jnp.logical_not(begins)
    here_odd = dot(one_hot(odd & here), windows)
    here_even = dot(one_hot(jnp.logical_not(odd) & here), windows)
    prev_even = dot(one_hot(jnp.logical_not(odd) & before), windows)
    lane = iota((frames, WIDE), 1)
    patches = pltpu.roll(here_odd, WIDE - PITCH, 1) + pltpu.roll(
        jnp.where(lane < 5 * PITCH, here_even, prev_even), 3 * PITCH, 1
    )
    for index, mel_bin in enumerate(BIN_ORDER):
        moved = patches if mel_bin == 0 else pltpu.roll(patches, WIDE - 2 * mel_bin, 1)
        patch_ref[index * frames : (index + 1) * frames, :] = moved.astype(BF16)
    tap_lane, tap_at = iota((WIDE, 16), 0), iota((WIDE, 16), 1)
    all_rows = BINS_IN * frames
    for row_tap in range(3):
        spread = (2 * row_tap + tap_at // 3) * PITCH + tap_at % 3
        weight = dot(one_hot((tap_lane == spread) & (tap_at < 9)), conv1_ref[...]).astype(BF16)
        for start in range(0, all_rows, 512):
            stop = min(start + 512, all_rows)
            response = dot(patch_ref[start:stop, :], weight)
            first_ref[row_tap, start:stop, :] = jnp.maximum(response, 0.0).astype(BF16)
    whole_rows = (1, EVENS + 1, 2)
    half_rows = (0, EVENS, 1)
    bin_a = jnp.where(share == 0, 5, 0)
    bin_b = jnp.where(share == 3, 0, 5)
    side_a = jnp.where((share == 1) | (share == 2), 1, 0)
    side_b = jnp.where((share == 0) | (share == 3), 1, 0)
    half = channels // 2
    for copy in conv2_copies:
        copy.wait()
    for begin in range(0, frames, CONV_ROWS):
        for part in range(FULL):
            total = None
            for tap in range(taps):
                at = (whole_rows[tap % 3] + part) * frames + begin
                product = dot(first_ref[tap // 3, at : at + CONV_ROWS, :], conv2_ref[tap])
                total = product if total is None else total + product
            columns = slice(part * channels, (part + 1) * channels)
            out_ref[begin : begin + CONV_ROWS, columns] = jnp.maximum(total, 0.0).astype(BF16)
        for index, (mel_bin, side) in enumerate(((bin_a, side_a), (bin_b, side_b))):
            columns = pl.ds(pl.multiple_of(side * half, 128), half)
            total = None
            for tap in range(taps):
                at = (half_rows[tap % 3] + mel_bin) * frames + begin
                rows = pl.ds(pl.multiple_of(at, 128), CONV_ROWS)
                product = dot(first_ref[tap // 3, rows, :], conv2_ref[tap, :, columns])
                total = product if total is None else total + product
            first = FULL * channels + index * half
            columns = slice(first, first + half)
            out_ref[begin : begin + CONV_ROWS, columns] = jnp.maximum(total, 0.0).astype(BF16)


def conv_features(place, lengths, blocks, conv1_weight, conv2_weight, frames):
    taps, channels, _ = conv2_weight.shape
    return pl.pallas_call(
        conv_kernel,
        out_shape=jax.ShapeDtypeStruct((frames, BINS * channels), BF16),
        in_specs=[SMEM] * 2 + [VMEM] * 5 + [HBM],
        out_specs=VMEM,
        scratch_shapes=[
            pltpu.VMEM(conv2_weight.shape, BF16),
            pltpu.VMEM((BINS_IN * frames, WIDE), BF16),
            pltpu.VMEM((3, BINS_IN * frames, channels), BF16),
            pltpu.SemaphoreType.DMA((taps,)),
        ],
        compiler_params=pltpu.CompilerParams(vmem_limit_bytes=48 * 1024 * 1024),
        name="convolutions",
    )(place, lengths, *blocks, conv1_weight, conv2_weight)


def proj_kernel(place_ref, features_ref, same_hbm, other_hbm, *refs):
    out_refs, (result_ref, proj_ref, sems) = refs[:-3], refs[-3:]
    group, seat = place_ref[0], place_ref[1]
    start, wait = proj_copies(group % 2, same_hbm, other_hbm, proj_ref, sems)
    start()
    zero_rims(proj_ref, same_hbm.shape[0])

    def features(column, size):
        return features_ref[:, column : column + size]

    result = project(features, seat ^ (group // 16), proj_ref, wait)
    result_ref[...] = result.astype(BF16)
    count = result_ref.shape[0]
    own = count // len(out_refs)
    for step, out_ref in enumerate(out_refs):
        for at in range(0, own + 2 * RIM, RIM):
            source = (step * own - RIM + at) % count
            out_ref[at : at + RIM, :] = result_ref[source : source + RIM, :]


def projected_chunks(place, features, proj, seats):
    rows, half = proj[0].shape
    frames = features.shape[0]
    shape = jax.ShapeDtypeStruct((frames // seats + 2 * RIM, 2 * half), BF16)
    return pl.pallas_call(
        proj_kernel,
        out_shape=[shape] * seats,
        in_specs=[SMEM, VMEM, HBM, HBM],
        out_specs=[VMEM] * seats,
        scratch_shapes=[
            pltpu.VMEM((frames, 2 * half), BF16),
            pltpu.VMEM((rows + 256, 2 * half), BF16),
            pltpu.SemaphoreType.DMA((2 * PROJ_PARTS,)),
        ],
        compiler_params=pltpu.CompilerParams(vmem_limit_bytes=40 * 1024 * 1024),
        name="projection",
    )(place, features, *proj)


def layer_norm(values):
    average = jnp.mean(values, axis=-1, keepdims=True)
    centered = values - average
    inverse = lax.rsqrt(jnp.mean(centered * centered, axis=-1, keepdims=True) + 1e-05)
    return centered * inverse, inverse


def norm_back(d_normed, normed, inverse):
    return (
        d_normed
        - jnp.mean(d_normed, axis=-1, keepdims=True)
        - normed * jnp.mean(d_normed * normed, axis=-1, keepdims=True)
    ) * inverse


def depthwise(source, seg_ref, taps_ref, moved_ref, out_ref, base, seg_base, count, reverse):
    kernel, width = taps_ref.shape
    half = (kernel - 1) // 2
    length = source.shape[0]
    for residue in range(8):
        for index in range(width // 128):
            lanes = slice(index * 128, (index + 1) * 128)
            column = source[:, lanes]
            if residue:
                column = pltpu.roll(column, length - residue, 0)
            moved_ref[residue, 0:length, lanes] = column
    step = 32
    for begin in range(0, count, step):
        mine = seg_ref[0, seg_base + begin : seg_base + begin + step, :]
        running = [jnp.zeros((step, 128), F32) for _ in range(width // 128)]
        for offset in range(kernel):
            shift = half - offset if reverse else offset - half
            residue = shift % 8
            other = seg_base + begin + shift - residue
            same = seg_ref[residue, other : other + step, :] == mine
            at = base + begin + shift - residue
            for index in range(width // 128):
                lanes = slice(index * 128, (index + 1) * 128)
                window = jnp.where(same, moved_ref[residue, at : at + step, lanes], 0.0)
                running[index] = running[index] + window * taps_ref[offset : offset + 1, lanes]
        for index in range(width // 128):
            out_ref[begin : begin + step, index * 128 : (index + 1) * 128] = running[index]


def module_kernel(
    place_ref,
    lengths_ref,
    part_0_ref,
    part_1_ref,
    part_2_ref,
    part_3_ref,
    cot_low_ref,
    cot_ref,
    cot_high_ref,
    gain_in_ref,
    point_in_ref,
    taps_ref,
    gain_mid_ref,
    point_out_ref,
    encoded_ref,
    grad_ref,
    glu_ref,
    seg_ref,
    mixed_ref,
    back_ref,
):
    own, width = cot_ref.shape
    total = own + 2 * RIM
    inner = own + RIM
    skip = RIM // 2
    encoder = part_0_ref[...].astype(F32) + part_1_ref[...].astype(F32)
    encoder = encoder + part_2_ref[...].astype(F32) + part_3_ref[...].astype(F32)
    encoder = encoder.astype(BF16).astype(F32)
    normed_in, inv_in = layer_norm(encoder)
    ln_in = (normed_in * gain_in_ref[...]).astype(BF16)
    left = dot(ln_in, point_in_ref[:, 0:width])
    gate = jax.nn.sigmoid(dot(ln_in, point_in_ref[:, width : 2 * width]))
    glu_out = (left * gate).astype(BF16).astype(F32)
    frame = place_ref[1] * own - RIM + iota((total, 128), 0)
    block = (frame + 4 * RIM) // 2 - 2 * RIM
    second = lengths_ref[0]
    third = second + lengths_ref[1]
    ends = third + lengths_ref[2]
    seg = (
        jnp.where(block >= 0, 1, 0)
        + jnp.where(block >= second, 1, 0)
        + jnp.where(block >= third, 1, 0)
        + jnp.where(block >= ends, 1, 0)
    )
    for residue in range(8):
        seg_ref[residue] = pltpu.roll(seg, total - residue, 0) if residue else seg
    depthwise(glu_out, seg_ref, taps_ref, glu_ref, mixed_ref, skip, skip, inner, False)
    normed_mid, inv_mid = layer_norm(mixed_ref[...])
    scaled = normed_mid * gain_mid_ref[...]
    logistic = jax.nn.sigmoid(scaled)
    slope = logistic * (1.0 + scaled * (1.0 - logistic))
    low = RIM - skip
    hidden = (scaled * logistic)[low : low + own].astype(BF16)
    encoded = encoder[RIM : RIM + own] + dot(hidden, point_out_ref[...])
    encoded_ref[...] = encoded.astype(BF16)
    low_edge, high_edge = [
        jnp.concatenate([ref[64 + 16 * piece : 80 + 16 * piece, :] for piece in range(3)], axis=1)
        for ref in (cot_low_ref, cot_high_ref)
    ]
    cotangent = jnp.concatenate([low_edge, cot_ref[...], high_edge], axis=0)
    d_hidden = dot_cols(cotangent, point_out_ref[...])
    d_mixed = norm_back(d_hidden * slope * gain_mid_ref[...], normed_mid, inv_mid)
    d_mixed = d_mixed.astype(BF16).astype(F32)
    depthwise(d_mixed, seg_ref, taps_ref, glu_ref, back_ref, low, RIM, own, True)
    d_glu = back_ref[...]
    own_gate = gate[RIM : RIM + own]
    d_left = d_glu * own_gate
    d_right = d_left * left[RIM : RIM + own] * (1.0 - own_gate)
    d_normed = dot_cols(d_left.astype(BF16), point_in_ref[:, 0:width])
    d_normed = d_normed + dot_cols(d_right.astype(BF16), point_in_ref[:, width : 2 * width])
    own_normed = normed_in[RIM : RIM + own]
    back = norm_back(d_normed * gain_in_ref[...], own_normed, inv_in[RIM : RIM + own])
    grad_ref[...] = (cot_ref[...].astype(F32) + back).astype(BF16)


def conv_module(place, lengths, parts, cotangents, gain_in, point_in, taps, gain_mid, point_out):
    own, width = cotangents[1].shape
    inner = own + RIM
    shape = jax.ShapeDtypeStruct((own, width), BF16)
    return pl.pallas_call(
        module_kernel,
        out_shape=(shape, shape),
        in_specs=[SMEM, SMEM] + [VMEM] * 12,
        out_specs=(VMEM, VMEM),
        scratch_shapes=[
            pltpu.VMEM((8, own + 2 * RIM, width), F32),
            pltpu.VMEM((8, own + 2 * RIM, 128), jnp.int32),
            pltpu.VMEM((inner, width), F32),
            pltpu.VMEM((own, width), F32),
        ],
        compiler_params=pltpu.CompilerParams(vmem_limit_bytes=48 * 1024 * 1024),
        name="conv_module",
    )(place, lengths, *parts, *cotangents, gain_in[None], point_in, taps, gain_mid[None], point_out)
def send(place, frames, block_dest, proj_weight):
    blocks, width = frames.shape
    rows, columns = proj_weight.shape
    shape = jax.ShapeDtypeStruct((rows, columns // 2), BF16)
    return pl.pallas_call(
        send_kernel,
        out_shape=(jax.ShapeDtypeStruct((blocks, 2, width), BF16), shape, shape),
        in_specs=[SMEM, VMEM, VMEM, VMEM],
        out_specs=(VMEM, VMEM, VMEM),
        name="send",
    )(place, frames, block_dest, proj_weight)


def landing_slots(place, dest):
    groups, blocks = dest.shape
    return pl.pallas_call(
        landing_kernel,
        out_shape=jax.ShapeDtypeStruct((2, groups, blocks), BF16),
        in_specs=[SMEM, VMEM],
        out_specs=VMEM,
        name="landing",
    )(place, dest)


def cut_matrix(seats, width):
    mel_bins = width // BLK
    share, frame, mel = np.meshgrid(
        np.arange(seats), np.arange(BLK), np.arange(PITCH), indexing="ij"
    )
    source = MEL_STEP * share - MEL_LEAD + mel
    fits = (mel < MEL_KEEP) & (source >= 0) & (source < mel_bins)
    source = np.where(fits, frame * mel_bins + source, -1).reshape(-1)
    return jnp.asarray(np.arange(width)[:, None] == source[None, :], BF16)


def place_blocks(place, arrived, landing, cotangent, seats):
    blocks = landing.shape[2]
    rim_rows = 16 * cotangent.shape[1] // WIDE
    rows = [blocks + (rim_rows if step in (1, seats - 1) else 0) for step in range(seats)]
    return pl.pallas_call(
        place_kernel,
        out_shape=[jax.ShapeDtypeStruct((count, WIDE), BF16) for count in rows],
        in_specs=[SMEM, VMEM, VMEM, VMEM, VMEM],
        out_specs=[VMEM] * seats,
        scratch_shapes=[pltpu.VMEM((blocks, seats * WIDE), BF16)],
        name="place",
    )(place, arrived, landing, cut_matrix(seats, arrived.shape[2]), cotangent)


def share_routes(groups, seats, flip):
    cluster = groups // seats
    routes = []
    for group in range(groups):
        for seat in range(seats):
            target = ((group // cluster) ^ seat) * cluster + (group % cluster ^ flip)
            routes.append((group * seats + seat, target * seats + seat))
    return routes


def gather_share(pair, groups, cluster):
    members = [
        [begin + core + 2 * index for index in range(cluster // 2)]
        for begin in range(0, groups, cluster)
        for core in range(2)
    ]
    rows, half = pair.shape
    copies = jnp.broadcast_to(pair[None], (cluster // 2, rows, half))
    same = lax.all_to_all(
        copies, "dp", split_axis=0, concat_axis=0, tiled=True, axis_index_groups=members
    ).reshape(-1, half)
    return same


def local(
    loader_frames,
    block_dest,
    utt_lengths,
    conv1_weight,
    conv2_weight,
    proj_weight,
    gain_in,
    point_in,
    taps,
    gain_mid,
    point_out,
    grad_encoded,
):
    groups, seats = lax.axis_size("dp"), lax.axis_size("seq")
    group, seat = lax.axis_index("dp"), lax.axis_index("seq")
    place = jnp.stack([group, seat]).astype(jnp.int32)
    lengths = utt_lengths[0]
    frames = loader_frames[0]
    blocks = frames.shape[0]
    cotangent = grad_encoded[0]
    own, width = cotangent.shape
    channels = conv2_weight.shape[1]
    rows = proj_weight.shape[0]
    cluster = groups // seats
    half = width // 2
    core = group % 2
    outgoing, same, other = send(place, frames, block_dest, proj_weight)
    same = lax.ppermute(same, ("dp", "seq"), share_routes(groups, seats, 0))
    other = lax.ppermute(other, ("dp", "seq"), share_routes(groups, seats, 1))
    arrived = lax.all_to_all(outgoing, "dp", split_axis=0, concat_axis=0, tiled=True)
    landing = landing_slots(place, block_dest.reshape(groups, blocks))
    windows = place_blocks(place, arrived, landing, cotangent, seats)
    pair = jnp.where(
        core == 0,
        jnp.concatenate([same, other], axis=0),
        jnp.concatenate([other, same], axis=0),
    )

    def ring(step):
        return [(index, (index + step) % seats) for index in range(seats)]

    windows = [windows[0]] + [
        lax.ppermute(windows[step], "seq", ring(step)) for step in range(1, seats)
    ]
    pair, _ = lax.optimization_barrier((pair, windows[1]))
    same = gather_share(pair, groups, cluster)
    conv1 = jnp.pad(conv1_weight, ((0, 16 - conv1_weight.shape[0]), (0, 0)))
    features = conv_features(place, lengths, windows, conv1, conv2_weight, seats * own)
    features, same = lax.optimization_barrier((features, same))
    other = lax.ppermute(same, "dp", [(index, index ^ 1) for index in range(groups)])
    parts = projected_chunks(place, features, (same, other), seats)
    parts = [parts[0]] + [
        lax.ppermute(parts[step], "seq", ring(step)) for step in range(1, seats)
    ]
    encoded, grad_input = conv_module(
        place,
        lengths,
        parts,
        (windows[1], cotangent, windows[3]),
        gain_in,
        point_in,
        taps,
        gain_mid,
        point_out,
    )
    return encoded[None], grad_input[None]


def solution(mesh):
    placed = (
        P("seq", "dp", None),
        P("seq", None),
        P("dp", None),
        P(),
        P(),
        P("dp", None),
        P(),
        P(),
        P(),
        P(),
        P(),
        P("dp", "seq", None),
    )
    return jax.shard_map(
        local,
        mesh=mesh,
        in_specs=placed,
        out_specs=(P("dp", "seq", None), P("dp", "seq", None)),
        check_vma=False,
    )
```

profile of v0, /device:TPU:1, one launch (start us, length us, event | category | flops | bytes accessed | tf_op | source)
XLA Modules:
  0.0 105.2 jit_solution(18415223956113792166)
XLA Ops:
  0.6 0.6 pad_add_fusion.place_ref
  1.3 2.1 %send.1 = (bf16[64,2,640]{2,1,0:T(2,128)(2,1)}, bf16[152,384]{1,0:T(8,128)(2,1)}, bf16[152,384]{1,0:T(8,128)(2,1)}) custom-call(s32[2]{0:T(128)} %pad_add_fusion.place_ref, bf16[64,640]{1,0:T(8,128)(2,1)} %bitcast.12, s32[1,4096]{1,0:T(1,128)} %dest_ref.1, bf16[152,768]{1,0:T(8,128)(2,1)} %proj_ref.1), custom_call_target="tpu_custom_call" | custom-call | tf_op jit(solution)/shard_map/send/pallas_call | solution.py:443
  3.3 13.2 %all-to-all-start = ((bf16[64,2,640]{2,1,0:T(2,128)(2,1)}), bf16[64,2,640]{2,1,0:T(2,128)(2,1)S(1)}, u32[]{:S(2)}, u32[]{:S(2)}) async-start(bf16[64,2,640]{2,1,0:T(2,128)(2,1)} %get-tuple-element.18), calls=%async_computation | async-start | bytes 327680 | tf_op jit(solution)/shard_map/all_to_all | solution.py:542
  16.5 1.6 %collective-permute-start.3 = (bf16[152,384]{1,0:T(8,128)(2,1)}, bf16[152,384]{1,0:T(8,128)(2,1)S(1)}, u32[]{:S(2)}, u32[]{:S(2)}) collective-permute-start(bf16[152,384]{1,0:T(8,128)(2,1)} %get-tuple-element.23), channel_id=1, source_target_pairs={{0,0},{1,65},{2,130},{3,195},{4,4},{5,69},{6,134},{7,199},{8,8},{9... | collective-permute-start | bytes 350216 | tf_op jit(solution)/shard_map/ppermute | solution.py:540
  18.0 0.5 collective-permute-start.4
  18.5 0.5 broadcast.7
  19.0 1.3 %reduce.3 = s32[4096]{0:T(1024)S(1)} reduce(s32[1,4096]{1,0:T(1,128)} %dest_ref.1, s32[]{:T(128)} %broadcast.7), dimensions={0}, to_apply=%param.14.reduce_sub_computation.3 | reduce | bytes 32772 | tf_op args[1]
  20.3 0.7 reshape.11.dest_ref
  21.0 1.6 %landing.1.landing_ref = bf16[2,64,64]{2,1,0:T(8,128)(2,1)} custom-call(s32[2]{0:T(128)} %pad_add_fusion.place_ref, s32[64,64]{1,0:T(8,128)} %reshape.11.dest_ref), custom_call_target="tpu_custom_call" | custom-call | tf_op jit(solution)/shard_map/landing/pallas_call | solution.py:454
  22.6 5.6 %all-to-all-done.arrived_ref = bf16[64,2,640]{2,1,0:T(2,128)(2,1)S(1)} async-done(((bf16[64,2,640]{2,1,0:T(2,128)(2,1)}), bf16[64,2,640]{2,1,0:T(2,128)(2,1)S(1)}, u32[]{:S(2)}, u32[]{:S(2)}) %all-to-all-start) | async-done | bytes 163872 | tf_op jit(solution)/shard_map/all_to_all | solution.py:542
  28.2 0.0 copy-start.7
  28.2 0.7 copy-done.7
  28.8 2.9 %place.1 = (bf16[64,256]{1,0:T(8,128)(2,1)}, bf16[112,256]{1,0:T(8,128)(2,1)}, bf16[64,256]{1,0:T(8,128)(2,1)}, bf16[112,256]{1,0:T(8,128)(2,1)}) custom-call(s32[2]{0:T(128)} %pad_add_fusion.place_ref, bf16[64,2,640]{2,1,0:T(2,128)(2,1)} %copy-done.7, bf16[2,64,64]{2,1,0:T(8,128)(2,1)} %landing.1.landing_ref, bf16[640,1024]{1,0:T(8,128)(2,1)} %constant.27.clone.cut_ref, ...), custom_call_target="tpu_custom_call" | custom-call | tf_op jit(solution)/shard_map/place/pallas_call | solution.py:478
  31.7 1.2 %collective-permute-start = (bf16[112,256]{1,0:T(8,128)(2,1)}, bf16[112,256]{1,0:T(8,128)(2,1)S(1)}, u32[]{:S(2)}, u32[]{:S(2)}) collective-permute-start(bf16[112,256]{1,0:T(8,128)(2,1)} %get-tuple-element.20), channel_id=1, source_target_pairs={{0,1},{1,2},{2,3},{3,0},{4,5},{5,6},{6,7},{7,4},{8,9},{9,10},{10,1... | collective-permute-start | bytes 172040 | tf_op jit(solution)/shard_map/ppermute | solution.py:555
  33.0 0.0 collective-permute-done.3
  33.0 0.0 collective-permute-done.4
  33.0 0.1 maximum_select_fusion
  33.0 3.2 %collective-permute-done.refs_1_.cot_low_ref = bf16[112,256]{1,0:T(8,128)(2,1)S(1)} collective-permute-done((bf16[112,256]{1,0:T(8,128)(2,1)}, bf16[112,256]{1,0:T(8,128)(2,1)S(1)}, u32[]{:S(2)}, u32[]{:S(2)}) %collective-permute-start) | collective-permute-done | bytes 57376 | tf_op jit(solution)/shard_map/ppermute | solution.py:555
  36.2 1.4 %broadcast_in_dim.18 = bf16[8,304,384]{2,1,0:T(8,128)(2,1)} broadcast(bf16[304,384]{1,0:T(8,128)(2,1)S(1)} %maximum_select_fusion), dimensions={1,2} | broadcast | bytes 2101248 | tf_op jit(solution)/shard_map/broadcast_in_dim | solution.py:505
  37.6 0.0 copy-start.11
  37.6 0.0 copy-start.12
  37.6 0.0 copy-start.8
  37.6 0.0 copy-start.4
  37.6 0.0 copy-start.5
  37.6 0.0 copy-start.6
  37.6 4.5 %all-to-all-start.1 = ((bf16[8,304,384]{2,1,0:T(8,128)(2,1)}), bf16[8,304,384]{2,1,0:T(8,128)(2,1)}, u32[]{:S(2)}, u32[]{:S(2)}) async-start(bf16[8,304,384]{2,1,0:T(8,128)(2,1)} %broadcast_in_dim.18), calls=%async_computation.1 | async-start | bytes 3735552 | tf_op jit(solution)/shard_map/all_to_all | solution.py:506
  42.1 0.0 copy-done.11
  42.1 1.5 %collective-permute-start.2 = (bf16[112,256]{1,0:T(8,128)(2,1)S(1)}, bf16[112,256]{1,0:T(8,128)(2,1)S(1)}, u32[]{:S(2)}, u32[]{:S(2)}) collective-permute-start(bf16[112,256]{1,0:T(8,128)(2,1)S(1)} %copy-done.11), channel_id=1, source_target_pairs={{0,3},{1,0},{2,1},{3,2},{4,7},{5,4},{6,5},{7,6},{8,11},{9,8},{10,9... | collective-permute-start | bytes 172040 | tf_op jit(solution)/shard_map/ppermute | solution.py:555
  43.6 0.0 copy-done.12
  43.6 2.0 %collective-permute-start.1 = (bf16[64,256]{1,0:T(8,128)(2,1)S(1)}, bf16[64,256]{1,0:T(8,128)(2,1)S(1)}, u32[]{:S(2)}, u32[]{:S(2)}) collective-permute-start(bf16[64,256]{1,0:T(8,128)(2,1)S(1)} %copy-done.12), channel_id=1, source_target_pairs={{0,2},{1,3},{2,0},{3,1},{4,6},{5,7},{6,4},{7,5},{8,10},{9,11},{10,... | collective-permute-start | bytes 98312 | tf_op jit(solution)/shard_map/ppermute | solution.py:555
  45.6 0.0 copy-done.8
  45.6 2.2 %collective-permute-done.1.refs_2_ = bf16[64,256]{1,0:T(8,128)(2,1)S(1)} collective-permute-done((bf16[64,256]{1,0:T(8,128)(2,1)S(1)}, bf16[64,256]{1,0:T(8,128)(2,1)S(1)}, u32[]{:S(2)}, u32[]{:S(2)}) %collective-permute-start.1) | collective-permute-done | bytes 32800 | tf_op jit(solution)/shard_map/ppermute | solution.py:555
  47.9 0.0 collective-permute-done.2.refs_3_.cot_high_ref
  47.9 0.0 copy-done.4
  47.9 0.0 copy-done.5
  47.9 0.0 copy-done.6
  47.9 19.7 %convolutions.1.features_ref = bf16[512,2560]{1,0:T(8,128)(2,1)S(1)} custom-call(s32[2]{0:T(128)S(1)} %copy-done.5, s32[3]{0:T(128)S(1)} %bitcast.10, bf16[64,256]{1,0:T(8,128)(2,1)S(1)} %copy-done.4, bf16[112,256]{1,0:T(8,128)(2,1)S(1)} %collective-permute-done.refs_1_.cot_low_ref, bf16[64,256]{1,0:T(8,128)(2,1)S(1)} %collective-permute-done.1.refs_2_, ...), custom_call_target="tpu_custom_call" | custom-call | tf_op jit(solution)/shard_map/convolutions/pallas_call | solution.py:246
  67.6 0.0 all-to-all-done.1
  67.6 0.0 copy-start.9
  67.6 0.0 copy-start.10
  67.6 0.0 copy-start
  67.6 0.0 copy-start.1
  67.6 0.0 copy-start.2
  67.6 0.0 copy-start.3
  67.6 4.4 %collective-permute-start.5 = (bf16[2432,384]{1,0:T(8,128)(2,1)}, bf16[2432,384]{1,0:T(8,128)(2,1)S(1)}, u32[]{:S(2)}, u32[]{:S(2)}) collective-permute-start(bf16[2432,384]{1,0:T(8,128)(2,1)} %bitcast.5.same_hbm), channel_id=1, source_target_pairs={{0,4},{4,0},{8,12},{12,8},{16,20},{20,16},{24,28},{28,24},{32,36},... | collective-permute-start | bytes 5603336 | tf_op jit(solution)/shard_map/ppermute | solution.py:562
  72.1 3.7 %collective-permute-done.5.other_hbm = bf16[2432,384]{1,0:T(8,128)(2,1)S(1)} collective-permute-done((bf16[2432,384]{1,0:T(8,128)(2,1)}, bf16[2432,384]{1,0:T(8,128)(2,1)S(1)}, u32[]{:S(2)}, u32[]{:S(2)}) %collective-permute-start.5) | collective-permute-done | bytes 1867808 | tf_op jit(solution)/shard_map/ppermute | solution.py:562
  75.7 5.0 %projection.1 = (bf16[192,768]{1,0:T(8,128)(2,1)S(1)}, bf16[192,768]{1,0:T(8,128)(2,1)S(1)}, bf16[192,768]{1,0:T(8,128)(2,1)S(1)}, bf16[192,768]{1,0:T(8,128)(2,1)S(1)}) custom-call(s32[2]{0:T(128)S(1)} %copy-done.5, bf16[512,2560]{1,0:T(8,128)(2,1)S(1)} %convolutions.1.features_ref, bf16[2432,384]{1,0:T(8,128)(2,1)} %bitcast.5.same_hbm, ...), custom_call_target="tpu_custom_call" | custom-call | tf_op jit(solution)/shard_map/projection/pallas_call | solution.py:286
  80.8 0.1 collective-permute-start.6
  80.9 1.3 %collective-permute-start.7 = (bf16[192,768]{1,0:T(8,128)(2,1)S(1)}, bf16[192,768]{1,0:T(8,128)(2,1)S(1)}, u32[]{:S(2)}, u32[]{:S(2)}) collective-permute-start(bf16[192,768]{1,0:T(8,128)(2,1)S(1)} %get-tuple-element.30), channel_id=1, source_target_pairs={{0,2},{1,3},{2,0},{3,1},{4,6},{5,7},{6,4},{7,5},{8,10},{9,11},{10,... | collective-permute-start | bytes 884744 | tf_op jit(solution)/shard_map/ppermute | solution.py:565
  82.2 1.3 %collective-permute-start.8 = (bf16[192,768]{1,0:T(8,128)(2,1)S(1)}, bf16[192,768]{1,0:T(8,128)(2,1)S(1)}, u32[]{:S(2)}, u32[]{:S(2)}) collective-permute-start(bf16[192,768]{1,0:T(8,128)(2,1)S(1)} %get-tuple-element.31), channel_id=1, source_target_pairs={{0,3},{1,0},{2,1},{3,2},{4,7},{5,4},{6,5},{7,6},{8,11},{9,8},{10,9... | collective-permute-start | bytes 884744 | tf_op jit(solution)/shard_map/ppermute | solution.py:565
  83.5 0.0 copy-done.9
  83.5 0.0 copy-done.10
  83.6 13.1 %collective-permute-done.6.part_1_ref = bf16[192,768]{1,0:T(8,128)(2,1)S(1)} collective-permute-done((bf16[192,768]{1,0:T(8,128)(2,1)S(1)}, bf16[192,768]{1,0:T(8,128)(2,1)S(1)}, u32[]{:S(2)}, u32[]{:S(2)}) %collective-permute-start.6) | collective-permute-done | bytes 294944 | tf_op jit(solution)/shard_map/ppermute | solution.py:565
  96.7 0.0 collective-permute-done.7.part_2_ref
  96.7 0.3 collective-permute-done.8.part_3_ref
  97.0 0.0 copy-done
  97.0 0.0 copy-done.1
  97.0 0.0 copy-done.2
  97.0 0.0 copy-done.3
  97.0 8.2 %conv_module.1 = (bf16[128,768]{1,0:T(8,128)(2,1)}, bf16[128,768]{1,0:T(8,128)(2,1)}) custom-call(s32[2]{0:T(128)S(1)} %copy-done.5, s32[3]{0:T(128)S(1)} %bitcast.11, bf16[192,768]{1,0:T(8,128)(2,1)S(1)} %get-tuple-element.28.part_0_ref, bf16[192,768]{1,0:T(8,128)(2,1)S(1)} %collective-permute-done.6.part_1_ref, ...), custom_call_target="tpu_custom_call" | custom-call | tf_op jit(solution)/shard_map/conv_module/pallas_call | solution.py:425
  (3 shorter events, 0.0 us)
Async XLA Ops:
  3.3 24.9 %all-to-all-start = ((bf16[64,2,640]{2,1,0:T(2,128)(2,1)}), bf16[64,2,640]{2,1,0:T(2,128)(2,1)S(1)}, u32[]{:S(2)}, u32[]{:S(2)}) async-start(bf16[64,2,640]{2,1,0:T(2,128)(2,1)} %get-tuple-element.18), calls=%async_computation | async-start | bytes 327680 | tf_op jit(solution)/shard_map/all_to_all | solution.py:542
  16.5 16.5 %collective-permute-start.3 = (bf16[152,384]{1,0:T(8,128)(2,1)}, bf16[152,384]{1,0:T(8,128)(2,1)S(1)}, u32[]{:S(2)}, u32[]{:S(2)}) collective-permute-start(bf16[152,384]{1,0:T(8,128)(2,1)} %get-tuple-element.23), channel_id=1, source_target_pairs={{0,0},{1,65},{2,130},{3,195},{4,4},{5,69},{6,134},{7,199},{8,8},{9... | collective-permute-start | bytes 350216 | tf_op jit(solution)/shard_map/ppermute | solution.py:540
  18.0 14.9 %collective-permute-start.4 = (bf16[152,384]{1,0:T(8,128)(2,1)}, bf16[152,384]{1,0:T(8,128)(2,1)S(1)}, u32[]{:S(2)}, u32[]{:S(2)}) collective-permute-start(bf16[152,384]{1,0:T(8,128)(2,1)} %get-tuple-element.24), channel_id=1, source_target_pairs={{0,4},{1,69},{2,134},{3,199},{4,0},{5,65},{6,130},{7,195},{8,12},{... | collective-permute-start | bytes 350216 | tf_op jit(solution)/shard_map/ppermute | solution.py:541
  28.2 0.7 copy-start.7
  31.7 4.4 %collective-permute-start = (bf16[112,256]{1,0:T(8,128)(2,1)}, bf16[112,256]{1,0:T(8,128)(2,1)S(1)}, u32[]{:S(2)}, u32[]{:S(2)}) collective-permute-start(bf16[112,256]{1,0:T(8,128)(2,1)} %get-tuple-element.20), channel_id=1, source_target_pairs={{0,1},{1,2},{2,3},{3,0},{4,5},{5,6},{6,7},{7,4},{8,9},{9,10},{10,1... | collective-permute-start | bytes 172040 | tf_op jit(solution)/shard_map/ppermute | solution.py:555
  37.6 4.5 %copy-start.11 = (bf16[112,256]{1,0:T(8,128)(2,1)S(1)}, bf16[112,256]{1,0:T(8,128)(2,1)}, u32[]{:S(2)}) copy-start(bf16[112,256]{1,0:T(8,128)(2,1)} %get-tuple-element.22) | copy-start | bytes 172036
  37.6 6.0 %copy-start.12 = (bf16[64,256]{1,0:T(8,128)(2,1)S(1)}, bf16[64,256]{1,0:T(8,128)(2,1)}, u32[]{:S(2)}) copy-start(bf16[64,256]{1,0:T(8,128)(2,1)} %get-tuple-element.21) | copy-start | bytes 98308
  37.6 8.1 %copy-start.8 = (bf16[9,512]{1,0:T(8,128)(2,1)S(1)}, bf16[9,512]{1,0:T(8,128)(2,1)}, u32[]{:S(2)}) copy-start(bf16[9,512]{1,0:T(8,128)(2,1)} %param.16) | copy-start | bytes 27652
  37.6 10.3 %copy-start.4 = (bf16[64,256]{1,0:T(8,128)(2,1)S(1)}, bf16[64,256]{1,0:T(8,128)(2,1)}, u32[]{:S(2)}) copy-start(bf16[64,256]{1,0:T(8,128)(2,1)} %get-tuple-element.19.refs_0_) | copy-start | bytes 98308
  37.6 10.3 %copy-start.5 = (s32[2]{0:T(128)S(1)}, s32[2]{0:T(128)}, u32[]{:S(2)}) copy-start(s32[2]{0:T(128)} %pad_add_fusion.place_ref) | copy-start | bytes 28
  37.6 10.3 %copy-start.6 = (s32[1,3]{1,0:T(1,128)S(1)}, s32[1,3]{1,0:T(1,128)}, u32[]{:S(2)}) copy-start(s32[1,3]{1,0:T(1,128)} %param.15) | copy-start | bytes 40
  37.6 29.9 %all-to-all-start.1 = ((bf16[8,304,384]{2,1,0:T(8,128)(2,1)}), bf16[8,304,384]{2,1,0:T(8,128)(2,1)}, u32[]{:S(2)}, u32[]{:S(2)}) async-start(bf16[8,304,384]{2,1,0:T(8,128)(2,1)} %broadcast_in_dim.18), calls=%async_computation.1 | async-start | bytes 3735552 | tf_op jit(solution)/shard_map/all_to_all | solution.py:506
  42.1 5.8 %collective-permute-start.2 = (bf16[112,256]{1,0:T(8,128)(2,1)S(1)}, bf16[112,256]{1,0:T(8,128)(2,1)S(1)}, u32[]{:S(2)}, u32[]{:S(2)}) collective-permute-start(bf16[112,256]{1,0:T(8,128)(2,1)S(1)} %copy-done.11), channel_id=1, source_target_pairs={{0,3},{1,0},{2,1},{3,2},{4,7},{5,4},{6,5},{7,6},{8,11},{9,8},{10,9... | collective-permute-start | bytes 172040 | tf_op jit(solution)/shard_map/ppermute | solution.py:555
  43.6 4.3 %collective-permute-start.1 = (bf16[64,256]{1,0:T(8,128)(2,1)S(1)}, bf16[64,256]{1,0:T(8,128)(2,1)S(1)}, u32[]{:S(2)}, u32[]{:S(2)}) collective-permute-start(bf16[64,256]{1,0:T(8,128)(2,1)S(1)} %copy-done.12), channel_id=1, source_target_pairs={{0,2},{1,3},{2,0},{3,1},{4,6},{5,7},{6,4},{7,5},{8,10},{9,11},{10,... | collective-permute-start | bytes 98312 | tf_op jit(solution)/shard_map/ppermute | solution.py:555
  67.6 16.0 %copy-start.9 = (f32[768]{0:T(1024)S(1)}, f32[768]{0:T(1024)}, u32[]{:S(2)}) copy-start(f32[768]{0:T(1024)} %param.19) | copy-start | bytes 9220
  67.6 16.0 %copy-start.10 = (f32[768]{0:T(1024)S(1)}, f32[768]{0:T(1024)}, u32[]{:S(2)}) copy-start(f32[768]{0:T(1024)} %param.22) | copy-start | bytes 9220
  67.6 29.4 %copy-start = (bf16[768,1536]{1,0:T(8,128)(2,1)S(1)}, bf16[768,1536]{1,0:T(8,128)(2,1)}, u32[]{:S(2)}) copy-start(bf16[768,1536]{1,0:T(8,128)(2,1)} %point_in_ref.1) | copy-start | bytes 7077892
  67.6 29.4 %copy-start.1 = (bf16[768,768]{1,0:T(8,128)(2,1)S(1)}, bf16[768,768]{1,0:T(8,128)(2,1)}, u32[]{:S(2)}) copy-start(bf16[768,768]{1,0:T(8,128)(2,1)} %point_out_ref.1) | copy-start | bytes 3538948
  67.6 29.4 %copy-start.2 = (bf16[1,128,768]{2,1,0:T(8,128)(2,1)S(1)}, bf16[1,128,768]{2,1,0:T(8,128)(2,1)}, u32[]{:S(2)}) copy-start(bf16[1,128,768]{2,1,0:T(8,128)(2,1)} %param.24) | copy-start | bytes 589828
  67.6 29.4 %copy-start.3 = (f32[31,768]{1,0:T(8,128)S(1)}, f32[31,768]{1,0:T(8,128)}, u32[]{:S(2)}) copy-start(f32[31,768]{1,0:T(8,128)} %taps_ref.1) | copy-start | bytes 285700
  67.6 8.1 %collective-permute-start.5 = (bf16[2432,384]{1,0:T(8,128)(2,1)}, bf16[2432,384]{1,0:T(8,128)(2,1)S(1)}, u32[]{:S(2)}, u32[]{:S(2)}) collective-permute-start(bf16[2432,384]{1,0:T(8,128)(2,1)} %bitcast.5.same_hbm), channel_id=1, source_target_pairs={{0,4},{4,0},{8,12},{12,8},{16,20},{20,16},{24,28},{28,24},{32,36},... | collective-permute-start | bytes 5603336 | tf_op jit(solution)/shard_map/ppermute | solution.py:562
  80.8 15.9 %collective-permute-start.6 = (bf16[192,768]{1,0:T(8,128)(2,1)S(1)}, bf16[192,768]{1,0:T(8,128)(2,1)S(1)}, u32[]{:S(2)}, u32[]{:S(2)}) collective-permute-start(bf16[192,768]{1,0:T(8,128)(2,1)S(1)} %get-tuple-element.29), channel_id=1, source_target_pairs={{0,1},{1,2},{2,3},{3,0},{4,5},{5,6},{6,7},{7,4},{8,9},{9,10},{10,1... | collective-permute-start | bytes 884744 | tf_op jit(solution)/shard_map/ppermute | solution.py:565
  80.9 15.8 %collective-permute-start.7 = (bf16[192,768]{1,0:T(8,128)(2,1)S(1)}, bf16[192,768]{1,0:T(8,128)(2,1)S(1)}, u32[]{:S(2)}, u32[]{:S(2)}) collective-permute-start(bf16[192,768]{1,0:T(8,128)(2,1)S(1)} %get-tuple-element.30), channel_id=1, source_target_pairs={{0,2},{1,3},{2,0},{3,1},{4,6},{5,7},{6,4},{7,5},{8,10},{9,11},{10,... | collective-permute-start | bytes 884744 | tf_op jit(solution)/shard_map/ppermute | solution.py:565
  82.2 14.8 %collective-permute-start.8 = (bf16[192,768]{1,0:T(8,128)(2,1)S(1)}, bf16[192,768]{1,0:T(8,128)(2,1)S(1)}, u32[]{:S(2)}, u32[]{:S(2)}) collective-permute-start(bf16[192,768]{1,0:T(8,128)(2,1)S(1)} %get-tuple-element.31), channel_id=1, source_target_pairs={{0,3},{1,0},{2,1},{3,2},{4,7},{5,4},{6,5},{7,6},{8,11},{9,8},{10,9... | collective-permute-start | bytes 884744 | tf_op jit(solution)/shard_map/ppermute | solution.py:565
where the time goes:
time: 106 us; the launch traced here: 105 us
  Pallas kernels  39.5 us (37%)
  starting transfers between devices  31.5 us (30%)
  waiting for transfers between devices  28.1 us (27%)
  local copies, waits for them, and re-layouts  3.3 us (3%)
  other arithmetic  1.99 us (2%)
    pallas_call x1, Pallas kernels, conv_features(): pl.pallas_call(conv_kernel, out_shape=jax.ShapeDtypeStruct((frames, BINS...  19.7 us
    ppermute x3, waiting for transfers between devices, local(): lax.ppermute(parts[step], 'seq', ring(step))  13.4 us
    all_to_all x1, starting transfers between devices, local(): lax.all_to_all(outgoing, 'dp', split_axis=0, concat_axis=0, tiled=True)  13.2 us
    pallas_call x1, Pallas kernels, conv_module(): pl.pallas_call(module_kernel, out_shape=(shape, shape), in_specs=[SMEM, S...  8.22 us
    all_to_all x1, waiting for transfers between devices, local(): lax.all_to_all(outgoing, 'dp', split_axis=0, concat_axis=0, tiled=True)  5.56 us
    ppermute x3, waiting for transfers between devices, local(): lax.ppermute(windows[step], 'seq', ring(step))  5.39 us
    pallas_call x1, Pallas kernels, projected_chunks(): pl.pallas_call(proj_kernel, out_shape=[shape] * seats, in_specs=[SMEM, VM...  5.04 us
    ppermute x3, starting transfers between devices, local(): lax.ppermute(windows[step], 'seq', ring(step))  4.74 us
  transfers between devices with their start and end apart: 11, of which 6 were waited for; matrix products, arithmetic and copies ran while one was open for 2% of the time, Pallas kernels for 23%

commit v1 on v0

--- a/solution.py
+++ b/solution.py
@@ -72,8 +72,13 @@
 
 def landing_kernel(place_ref, dest_ref, out_ref):
     group = place_ref[0]
-    groups, blocks = dest_ref.shape
-    dest = dest_ref[...]
+    _, groups, blocks = out_ref.shape
+    rows = [dest_ref[:, at : at + 128] for at in range(0, groups * blocks, 128)]
+    dest = jnp.concatenate(rows, axis=0)
+    dest = jnp.concatenate([dest, pltpu.roll(dest, 128 - blocks, 1)], axis=0)[:, 0:blocks]
+    at_row, at_col = iota((groups, groups), 0), iota((groups, groups), 1)
+    pairs = groups // 2
+    order = one_hot(at_row == jnp.where(at_col < pairs, 2 * at_col, 2 * (at_col - pairs) + 1))
     mine = dest // blocks == group
     earlier = one_hot(iota((blocks, blocks), 0) < iota((blocks, blocks), 1))
     rank = dot(one_hot(mine), earlier)
@@ -81,7 +86,8 @@
     for copy in range(2):
         kept = jnp.where(mine & (rank == float(copy)), spot + 1, 0)
         landing = jnp.sum(kept, axis=1, keepdims=True) - 1
-        out_ref[copy] = one_hot(iota((groups, blocks), 1) == landing)
+        landing = one_hot(iota((groups, blocks), 1) == landing)
+        out_ref[copy] = dot(order, landing).astype(BF16)
 
 
 def place_kernel(place_ref, arrived_ref, landing_ref, cut_ref, cot_ref, *out_refs):
@@ -113,33 +119,13 @@
     return 128 * share + 128, start_a, start_b
 
 
-def proj_copies(core, same_hbm, other_hbm, proj_ref, sems):
-    rows, half = same_hbm.shape
-    parts = sems.shape[0] // 2
-    size = rows // parts
-
-    def copy(here, part, side):
-        source = same_hbm if here == side else other_hbm
-        return pltpu.make_async_copy(
-            source.at[pl.ds(part * size, size)],
-            proj_ref.at[pl.ds(128 + part * size, size), pl.ds(side * half, half)],
-            sems.at[2 * part + side],
-        )
-
-    def start():
-        for here in range(2):
-
-            @pl.when(core == here)
-            def _():
-                for part in range(parts):
-                    for side in range(2):
-                        copy(here, part, side).start()
-
-    def wait(part):
-        for side in range(2):
-            copy(0, part, side).wait()
-
-    return start, wait
+def proj_copy(proj_hbm, proj_ref, sems, part):
+    size = proj_hbm.shape[0] // PROJ_PARTS
+    return pltpu.make_async_copy(
+        proj_hbm.at[pl.ds(part * size, size)],
+        proj_ref.at[pl.ds(128 + part * size, size)],
+        sems.at[part],
+    )
 
 
 def project(features, share, proj_ref, wait):
@@ -259,15 +245,18 @@
     )(place, lengths, *blocks, conv1_weight, conv2_weight)
 
 
-def proj_kernel(place_ref, features_ref, same_hbm, other_hbm, *refs):
+def proj_kernel(place_ref, features_ref, proj_hbm, *refs):
     out_refs, (result_ref, proj_ref, sems) = refs[:-3], refs[-3:]
     group, seat = place_ref[0], place_ref[1]
-    start, wait = proj_copies(group % 2, same_hbm, other_hbm, proj_ref, sems)
-    start()
-    zero_rims(proj_ref, same_hbm.shape[0])
+    for part in range(PROJ_PARTS):
+        proj_copy(proj_hbm, proj_ref, sems, part).start()
+    zero_rims(proj_ref, proj_hbm.shape[0])
 
     def features(column, size):
         return features_ref[:, column : column + size]
+
+    def wait(part):
+        proj_copy(proj_hbm, proj_ref, sems, part).wait()
 
     result = project(features, seat ^ (group // 16), proj_ref, wait)
     result_ref[...] = result.astype(BF16)
@@ -279,23 +268,23 @@
             out_ref[at : at + RIM, :] = result_ref[source : source + RIM, :]
 
 
-def projected_chunks(place, features, proj, seats):
-    rows, half = proj[0].shape
+def projected_parts(place, features, proj, seats):
+    rows, half = proj.shape
     frames = features.shape[0]
-    shape = jax.ShapeDtypeStruct((frames // seats + 2 * RIM, 2 * half), BF16)
+    shape = jax.ShapeDtypeStruct((frames // seats + 2 * RIM, half), BF16)
     return pl.pallas_call(
         proj_kernel,
         out_shape=[shape] * seats,
-        in_specs=[SMEM, VMEM, HBM, HBM],
+        in_specs=[SMEM, VMEM, HBM],
         out_specs=[VMEM] * seats,
         scratch_shapes=[
-            pltpu.VMEM((frames, 2 * half), BF16),
-            pltpu.VMEM((rows + 256, 2 * half), BF16),
-            pltpu.SemaphoreType.DMA((2 * PROJ_PARTS,)),
+            pltpu.VMEM((frames, half), BF16),
+            pltpu.VMEM((rows + 256, half), BF16),
+            pltpu.SemaphoreType.DMA((PROJ_PARTS,)),
         ],
         compiler_params=pltpu.CompilerParams(vmem_limit_bytes=40 * 1024 * 1024),
         name="projection",
-    )(place, features, *proj)
+    )(place, features, proj)
 
 
 def layer_norm(values):
@@ -345,10 +334,14 @@
 def module_kernel(
     place_ref,
     lengths_ref,
-    part_0_ref,
-    part_1_ref,
-    part_2_ref,
-    part_3_ref,
+    same_0_ref,
+    same_1_ref,
+    same_2_ref,
+    same_3_ref,
+    other_0_ref,
+    other_1_ref,
+    other_2_ref,
+    other_3_ref,
     cot_low_ref,
     cot_ref,
     cot_high_ref,
@@ -368,9 +361,13 @@
     total = own + 2 * RIM
     inner = own + RIM
     skip = RIM // 2
-    encoder = part_0_ref[...].astype(F32) + part_1_ref[...].astype(F32)
-    encoder = encoder + part_2_ref[...].astype(F32) + part_3_ref[...].astype(F32)
-    encoder = encoder.astype(BF16).astype(F32)
+    same = same_0_ref[...].astype(F32) + same_1_ref[...].astype(F32)
+    same = same + same_2_ref[...].astype(F32) + same_3_ref[...].astype(F32)
+    other = other_0_ref[...].astype(F32) + other_1_ref[...].astype(F32)
+    other = other + other_2_ref[...].astype(F32) + other_3_ref[...].astype(F32)
+    odd = place_ref[0] % 2 == 1
+    halves = [jnp.where(odd, other, same), jnp.where(odd, same, other)]
+    encoder = jnp.concatenate(halves, axis=1).astype(BF16).astype(F32)
     normed_in, inv_in = layer_norm(encoder)
     ln_in = (normed_in * gain_in_ref[...]).astype(BF16)
     left = dot(ln_in, point_in_ref[:, 0:width])
@@ -425,7 +422,7 @@
     return pl.pallas_call(
         module_kernel,
         out_shape=(shape, shape),
-        in_specs=[SMEM, SMEM] + [VMEM] * 12,
+        in_specs=[SMEM, SMEM] + [VMEM] * 16,
         out_specs=(VMEM, VMEM),
         scratch_shapes=[
             pltpu.VMEM((8, own + 2 * RIM, width), F32),
@@ -449,15 +446,14 @@
     )(place, frames, block_dest, proj_weight)
 
 
-def landing_slots(place, dest):
-    groups, blocks = dest.shape
+def landing_slots(place, block_dest, groups, blocks):
     return pl.pallas_call(
         landing_kernel,
         out_shape=jax.ShapeDtypeStruct((2, groups, blocks), BF16),
         in_specs=[SMEM, VMEM],
         out_specs=VMEM,
         name="landing",
-    )(place, dest)
+    )(place, block_dest)
 
 
 def cut_matrix(seats, width):
@@ -540,7 +536,7 @@
     same = lax.ppermute(same, ("dp", "seq"), share_routes(groups, seats, 0))
     other = lax.ppermute(other, ("dp", "seq"), share_routes(groups, seats, 1))
     arrived = lax.all_to_all(outgoing, "dp", split_axis=0, concat_axis=0, tiled=True)
-    landing = landing_slots(place, block_dest.reshape(groups, blocks))
+    landing = landing_slots(place, block_dest, groups, blocks)
     windows = place_blocks(place, arrived, landing, cotangent, seats)
     pair = jnp.where(
         core == 0,
@@ -554,16 +550,18 @@
     windows = [windows[0]] + [
         lax.ppermute(windows[step], "seq", ring(step)) for step in range(1, seats)
     ]
-    pair, _ = lax.optimization_barrier((pair, windows[1]))
+    pair, *windows = lax.optimization_barrier((pair, *windows))
     same = gather_share(pair, groups, cluster)
     conv1 = jnp.pad(conv1_weight, ((0, 16 - conv1_weight.shape[0]), (0, 0)))
     features = conv_features(place, lengths, windows, conv1, conv2_weight, seats * own)
     features, same = lax.optimization_barrier((features, same))
     other = lax.ppermute(same, "dp", [(index, index ^ 1) for index in range(groups)])
-    parts = projected_chunks(place, features, (same, other), seats)
-    parts = [parts[0]] + [
-        lax.ppermute(parts[step], "seq", ring(step)) for step in range(1, seats)
-    ]
+    parts = []
+    for proj in (same, other):
+        sums = projected_parts(place, features, proj, seats)
+        parts += [sums[0]] + [
+            lax.ppermute(sums[step], "seq", ring(step)) for step in range(1, seats)
+        ]
     encoded, grad_input = conv_module(
         place,
         lengths,

time: 106 us -> 98.7 us (0.931)
  waiting for transfers between devices: 28.1 us -> 20.6 us
  Pallas kernels: 39.5 us -> 41.6 us
  other arithmetic: 1.99 us -> 0.67 us
  local copies, waits for them, and re-layouts: 3.3 us -> 2.12 us
    ppermute x3 -> x6, waiting for transfers between devices: 13.4 us -> 6.94 us  [local(): lax.ppermute(sums[step], 'seq', ring(step))]
    ppermute x3 -> x6, starting transfers between devices: 2.75 us -> 6.75 us  [local(): lax.ppermute(sums[step], 'seq', ring(step))]
    ppermute x1, waiting for transfers between devices: 3.67 us -> 0.01 us  [local(): lax.ppermute(same, 'dp', [(index, index ^ 1) for index in range(groups)])]
    all_to_all x1, waiting for transfers between devices: 0.01 us -> 2.88 us  [gather_share(): lax.all_to_all(copies, 'dp', split_axis=0, concat_axis=0, tiled=True, axi...]
    ppermute x1, starting transfers between devices: 4.4 us -> 1.71 us  [local(): lax.ppermute(same, 'dp', [(index, index ^ 1) for index in range(groups)])]
    ppermute x3, waiting for transfers between devices: 5.39 us -> 2.89 us  [local(): lax.ppermute(windows[step], 'seq', ring(step))]
    all_to_all x1, waiting for transfers between devices: 5.56 us -> 7.93 us  [local(): lax.all_to_all(outgoing, 'dp', split_axis=0, concat_axis=0, tiled=True)]
    pallas_call x1 -> x2, Pallas kernels: 5.04 us -> 6.92 us  [projected_parts(): pl.pallas_call(proj_kernel, out_shape=[shape] * seats, in_specs=[SMEM, VM...]
  transfers between devices with their start and end apart: 11 -> 14, of which waited for: 6 -> 6; matrix products, arithmetic and copies ran while one was open for 2% -> 0% of each run, Pallas kernels for 23% -> 32%
where the time goes in v1:
time: 98.7 us; the launch traced here: 98.3 us
  Pallas kernels  41.6 us (42%)
  starting transfers between devices  32.5 us (33%)
  waiting for transfers between devices  20.6 us (21%)
  local copies, waits for them, and re-layouts  2.12 us (2%)
    pallas_call x1, Pallas kernels, conv_features(): pl.pallas_call(conv_kernel, out_shape=jax.ShapeDtypeStruct((frames, BINS...  19.7 us
    all_to_all x1, starting transfers between devices, local(): lax.all_to_all(outgoing, 'dp', split_axis=0, concat_axis=0, tiled=True)  13.2 us
    pallas_call x1, Pallas kernels, conv_module(): pl.pallas_call(module_kernel, out_shape=(shape, shape), in_specs=[SMEM, S...  8.26 us
    all_to_all x1, waiting for transfers between devices, local(): lax.all_to_all(outgoing, 'dp', split_axis=0, concat_axis=0, tiled=True)  7.93 us
    ppermute x6, waiting for transfers between devices, local(): lax.ppermute(sums[step], 'seq', ring(step))  6.94 us
    pallas_call x2, Pallas kernels, projected_parts(): pl.pallas_call(proj_kernel, out_shape=[shape] * seats, in_specs=[SMEM, VM...  6.92 us
    ppermute x6, starting transfers between devices, local(): lax.ppermute(sums[step], 'seq', ring(step))  6.75 us
    all_to_all x1, starting transfers between devices, gather_share(): lax.all_to_all(copies, 'dp', split_axis=0, concat_axis=0, tiled=True, axi...  4.64 us
  transfers between devices with their start and end apart: 14, of which 6 were waited for; matrix products, arithmetic and copies ran while one was open for 0% of the time, Pallas kernels for 32%

profile of v1, /device:TPU:1, one launch (start us, length us, event | category | flops | bytes accessed | tf_op | source)
XLA Modules:
  0.0 98.3 jit_solution(11868475574491952905)
XLA Ops:
  0.6 0.6 pad_add_fusion.place_ref
  1.2 2.1 %send.1 = (bf16[64,2,640]{2,1,0:T(2,128)(2,1)}, bf16[152,384]{1,0:T(8,128)(2,1)}, bf16[152,384]{1,0:T(8,128)(2,1)}) custom-call(s32[2]{0:T(128)} %pad_add_fusion.place_ref, bf16[64,640]{1,0:T(8,128)(2,1)} %bitcast.12, s32[1,4096]{1,0:T(1,128)} %dest_ref.3, bf16[152,768]{1,0:T(8,128)(2,1)} %proj_ref.1), custom_call_target="tpu_custom_call" | custom-call | tf_op jit(solution)/shard_map/send/pallas_call | solution.py:440
  3.3 13.2 %all-to-all-start = ((bf16[64,2,640]{2,1,0:T(2,128)(2,1)}), bf16[64,2,640]{2,1,0:T(2,128)(2,1)S(1)}, u32[]{:S(2)}, u32[]{:S(2)}) async-start(bf16[64,2,640]{2,1,0:T(2,128)(2,1)} %get-tuple-element.28), calls=%async_computation | async-start | bytes 327680 | tf_op jit(solution)/shard_map/all_to_all | solution.py:538
  16.5 1.6 %collective-permute-start = (bf16[152,384]{1,0:T(8,128)(2,1)}, bf16[152,384]{1,0:T(8,128)(2,1)S(1)}, u32[]{:S(2)}, u32[]{:S(2)}) collective-permute-start(bf16[152,384]{1,0:T(8,128)(2,1)} %get-tuple-element.26), channel_id=1, source_target_pairs={{0,0},{1,65},{2,130},{3,195},{4,4},{5,69},{6,134},{7,199},{8,8},{9... | collective-permute-start | bytes 350216 | tf_op jit(solution)/shard_map/ppermute | solution.py:536
  18.0 0.5 collective-permute-start.1
  18.5 1.7 %landing.1.landing_ref = bf16[2,64,64]{2,1,0:T(8,128)(2,1)} custom-call(s32[2]{0:T(128)} %pad_add_fusion.place_ref, s32[1,4096]{1,0:T(1,128)} %dest_ref.3), custom_call_target="tpu_custom_call" | custom-call | tf_op jit(solution)/shard_map/landing/pallas_call | solution.py:450
  20.2 7.9 %all-to-all-done.arrived_ref = bf16[64,2,640]{2,1,0:T(2,128)(2,1)S(1)} async-done(((bf16[64,2,640]{2,1,0:T(2,128)(2,1)}), bf16[64,2,640]{2,1,0:T(2,128)(2,1)S(1)}, u32[]{:S(2)}, u32[]{:S(2)}) %all-to-all-start) | async-done | bytes 163872 | tf_op jit(solution)/shard_map/all_to_all | solution.py:538
  28.2 0.0 copy-start.7
  28.2 0.7 copy-done.7
  28.8 2.9 %place.1 = (bf16[64,256]{1,0:T(8,128)(2,1)}, bf16[112,256]{1,0:T(8,128)(2,1)}, bf16[64,256]{1,0:T(8,128)(2,1)}, bf16[112,256]{1,0:T(8,128)(2,1)}) custom-call(s32[2]{0:T(128)} %pad_add_fusion.place_ref, bf16[64,2,640]{2,1,0:T(2,128)(2,1)} %copy-done.7, bf16[2,64,64]{2,1,0:T(8,128)(2,1)} %landing.1.landing_ref, bf16[640,1024]{1,0:T(8,128)(2,1)} %constant.27.clone.cut_ref, ...), custom_call_target="tpu_custom_call" | custom-call | tf_op jit(solution)/shard_map/place/pallas_call | solution.py:474
  31.7 1.2 %collective-permute-start.2 = (bf16[112,256]{1,0:T(8,128)(2,1)}, bf16[112,256]{1,0:T(8,128)(2,1)S(1)}, u32[]{:S(2)}, u32[]{:S(2)}) collective-permute-start(bf16[112,256]{1,0:T(8,128)(2,1)} %get-tuple-element.30), channel_id=1, source_target_pairs={{0,1},{1,2},{2,3},{3,0},{4,5},{5,6},{6,7},{7,4},{8,9},{9,10},{10,1... | collective-permute-start | bytes 172040 | tf_op jit(solution)/shard_map/ppermute | solution.py:551
  33.0 1.5 %collective-permute-start.4 = (bf16[112,256]{1,0:T(8,128)(2,1)}, bf16[112,256]{1,0:T(8,128)(2,1)S(1)}, u32[]{:S(2)}, u32[]{:S(2)}) collective-permute-start(bf16[112,256]{1,0:T(8,128)(2,1)} %get-tuple-element.32), channel_id=1, source_target_pairs={{0,3},{1,0},{2,1},{3,2},{4,7},{5,4},{6,5},{7,6},{8,11},{9,8},{10,9... | collective-permute-start | bytes 172040 | tf_op jit(solution)/shard_map/ppermute | solution.py:551
  34.4 1.5 %collective-permute-start.3 = (bf16[64,256]{1,0:T(8,128)(2,1)}, bf16[64,256]{1,0:T(8,128)(2,1)S(1)}, u32[]{:S(2)}, u32[]{:S(2)}) collective-permute-start(bf16[64,256]{1,0:T(8,128)(2,1)} %get-tuple-element.31), channel_id=1, source_target_pairs={{0,2},{1,3},{2,0},{3,1},{4,6},{5,7},{6,4},{7,5},{8,10},{9,11},{10,... | collective-permute-start | bytes 98312 | tf_op jit(solution)/shard_map/ppermute | solution.py:551
  36.0 0.0 collective-permute-done
  36.0 0.0 collective-permute-done.1
  36.0 0.1 maximum_select_fusion
  36.0 2.9 %collective-permute-done.3.refs_2_ = bf16[64,256]{1,0:T(8,128)(2,1)S(1)} collective-permute-done((bf16[64,256]{1,0:T(8,128)(2,1)}, bf16[64,256]{1,0:T(8,128)(2,1)S(1)}, u32[]{:S(2)}, u32[]{:S(2)}) %collective-permute-start.3) | collective-permute-done | bytes 32800 | tf_op jit(solution)/shard_map/ppermute | solution.py:551
  38.9 0.0 collective-permute-done.2.refs_1_.cot_low_ref
  38.9 0.0 collective-permute-done.4.refs_3_.cot_high_ref
  38.9 1.4 %broadcast_in_dim.18 = bf16[8,304,384]{2,1,0:T(8,128)(2,1)} broadcast(bf16[304,384]{1,0:T(8,128)(2,1)S(1)} %maximum_select_fusion), dimensions={1,2} | broadcast | bytes 2101248 | tf_op jit(solution)/shard_map/broadcast_in_dim | solution.py:501
  40.3 0.0 copy-start.8
  40.3 0.0 copy-start.4
  40.3 0.0 copy-start.5
  40.3 0.0 copy-start.6
  40.3 4.6 %all-to-all-start.1 = ((bf16[8,304,384]{2,1,0:T(8,128)(2,1)}), bf16[8,304,384]{2,1,0:T(8,128)(2,1)}, u32[]{:S(2)}, u32[]{:S(2)}) async-start(bf16[8,304,384]{2,1,0:T(8,128)(2,1)} %broadcast_in_dim.18), calls=%async_computation.1 | async-start | bytes 3735552 | tf_op jit(solution)/shard_map/all_to_all | solution.py:502
  45.0 0.0 copy-done.8
  45.0 0.0 copy-done.4
  45.0 0.0 copy-done.5
  45.0 0.0 copy-done.6
  45.0 19.7 %convolutions.1.features_ref = bf16[512,2560]{1,0:T(8,128)(2,1)S(1)} custom-call(s32[2]{0:T(128)S(1)} %copy-done.5, s32[3]{0:T(128)S(1)} %bitcast.10, bf16[64,256]{1,0:T(8,128)(2,1)S(1)} %copy-done.4, bf16[112,256]{1,0:T(8,128)(2,1)S(1)} %collective-permute-done.2.refs_1_.cot_low_ref, bf16[64,256]{1,0:T(8,128)(2,1)S(1)} %collective-permute-done.3.refs_2_, ...), custom_call_target="tpu_custom_call" | custom-call | tf_op jit(solution)/shard_map/convolutions/pallas_call | solution.py:232
  64.7 2.9 %all-to-all-done.1 = bf16[8,304,384]{2,1,0:T(8,128)(2,1)} async-done(((bf16[8,304,384]{2,1,0:T(8,128)(2,1)}), bf16[8,304,384]{2,1,0:T(8,128)(2,1)}, u32[]{:S(2)}, u32[]{:S(2)}) %all-to-all-start.1) | async-done | bytes 1867808 | tf_op jit(solution)/shard_map/all_to_all | solution.py:502
  67.6 1.7 %collective-permute-start.8 = (bf16[2432,384]{1,0:T(8,128)(2,1)}, bf16[2432,384]{1,0:T(8,128)(2,1)S(1)}, u32[]{:S(2)}, u32[]{:S(2)}) collective-permute-start(bf16[2432,384]{1,0:T(8,128)(2,1)} %bitcast.5.proj_hbm), channel_id=1, source_target_pairs={{0,4},{4,0},{8,12},{12,8},{16,20},{20,16},{24,28},{28,24},{32,36},... | collective-permute-start | bytes 5603336 | tf_op jit(solution)/shard_map/ppermute | solution.py:558
  69.3 3.5 %projection.2 = (bf16[192,384]{1,0:T(8,128)(2,1)S(1)}, bf16[192,384]{1,0:T(8,128)(2,1)S(1)}, bf16[192,384]{1,0:T(8,128)(2,1)S(1)}, bf16[192,384]{1,0:T(8,128)(2,1)S(1)}) custom-call(s32[2]{0:T(128)S(1)} %copy-done.5, bf16[512,2560]{1,0:T(8,128)(2,1)S(1)} %convolutions.1.features_ref, bf16[2432,384]{1,0:T(8,128)(2,1)} %bitcast.5.proj_hbm), custom_call_target="tpu_custom_call" | custom-call | tf_op jit(solution)/shard_map/projection/pallas_call | solution.py:275
  72.8 0.4 collective-permute-start.5
  73.2 2.2 %collective-permute-start.6 = (bf16[192,384]{1,0:T(8,128)(2,1)S(1)}, bf16[192,384]{1,0:T(8,128)(2,1)S(1)}, u32[]{:S(2)}, u32[]{:S(2)}) collective-permute-start(bf16[192,384]{1,0:T(8,128)(2,1)S(1)} %get-tuple-element.42), channel_id=1, source_target_pairs={{0,2},{1,3},{2,0},{3,1},{4,6},{5,7},{6,4},{7,5},{8,10},{9,11},{10,... | collective-permute-start | bytes 442376 | tf_op jit(solution)/shard_map/ppermute | solution.py:563
  75.5 0.0 copy-start.9
  75.5 0.0 copy-start.10
  75.5 0.0 copy-start
  75.5 0.0 copy-start.1
  75.5 0.0 copy-start.2
  75.5 0.0 copy-start.3
  75.5 1.1 %collective-permute-start.7 = (bf16[192,384]{1,0:T(8,128)(2,1)S(1)}, bf16[192,384]{1,0:T(8,128)(2,1)S(1)}, u32[]{:S(2)}, u32[]{:S(2)}) collective-permute-start(bf16[192,384]{1,0:T(8,128)(2,1)S(1)} %get-tuple-element.43), channel_id=1, source_target_pairs={{0,3},{1,0},{2,1},{3,2},{4,7},{5,4},{6,5},{7,6},{8,11},{9,8},{10,9... | collective-permute-start | bytes 442376 | tf_op jit(solution)/shard_map/ppermute | solution.py:563
  76.6 0.0 collective-permute-done.8.proj_hbm
  76.6 3.4 %projection.3 = (bf16[192,384]{1,0:T(8,128)(2,1)S(1)}, bf16[192,384]{1,0:T(8,128)(2,1)S(1)}, bf16[192,384]{1,0:T(8,128)(2,1)S(1)}, bf16[192,384]{1,0:T(8,128)(2,1)S(1)}) custom-call(s32[2]{0:T(128)S(1)} %copy-done.5, bf16[512,2560]{1,0:T(8,128)(2,1)S(1)} %convolutions.1.features_ref, bf16[2432,384]{1,0:T(8,128)(2,1)S(1)} %collective-permute-done.8.proj_hbm), custom_call_target="tpu_custom_call" | custom-call | tf_op jit(solution)/shard_map/projection/pallas_call | solution.py:275
  80.0 1.5 %collective-permute-start.10 = (bf16[192,384]{1,0:T(8,128)(2,1)S(1)}, bf16[192,384]{1,0:T(8,128)(2,1)S(1)}, u32[]{:S(2)}, u32[]{:S(2)}) collective-permute-start(bf16[192,384]{1,0:T(8,128)(2,1)S(1)} %get-tuple-element.46), channel_id=1, source_target_pairs={{0,2},{1,3},{2,0},{3,1},{4,6},{5,7},{6,4},{7,5},{8,10},{9,11},{10,... | collective-permute-start | bytes 442376 | tf_op jit(solution)/shard_map/ppermute | solution.py:563
  81.6 1.4 %collective-permute-start.11 = (bf16[192,384]{1,0:T(8,128)(2,1)S(1)}, bf16[192,384]{1,0:T(8,128)(2,1)S(1)}, u32[]{:S(2)}, u32[]{:S(2)}) collective-permute-start(bf16[192,384]{1,0:T(8,128)(2,1)S(1)} %get-tuple-element.47), channel_id=1, source_target_pairs={{0,3},{1,0},{2,1},{3,2},{4,7},{5,4},{6,5},{7,6},{8,11},{9,8},{10,9... | collective-permute-start | bytes 442376 | tf_op jit(solution)/shard_map/ppermute | solution.py:563
  82.9 0.0 collective-permute-done.5.same_1_ref
  83.0 0.1 collective-permute-start.9
  83.0 0.0 copy-done.9
  83.1 0.0 copy-done.10
  83.1 0.0 collective-permute-done.6.same_2_ref
  83.1 0.0 collective-permute-done.7.same_3_ref
  83.1 3.1 %collective-permute-done.10.other_2_ref = bf16[192,384]{1,0:T(8,128)(2,1)S(1)} collective-permute-done((bf16[192,384]{1,0:T(8,128)(2,1)S(1)}, bf16[192,384]{1,0:T(8,128)(2,1)S(1)}, u32[]{:S(2)}, u32[]{:S(2)}) %collective-permute-start.10) | collective-permute-done | bytes 147488 | tf_op jit(solution)/shard_map/ppermute | solution.py:563
  86.2 3.2 %collective-permute-done.11.other_3_ref = bf16[192,384]{1,0:T(8,128)(2,1)S(1)} collective-permute-done((bf16[192,384]{1,0:T(8,128)(2,1)S(1)}, bf16[192,384]{1,0:T(8,128)(2,1)S(1)}, u32[]{:S(2)}, u32[]{:S(2)}) %collective-permute-start.11) | collective-permute-done | bytes 147488 | tf_op jit(solution)/shard_map/ppermute | solution.py:563
  89.4 0.6 collective-permute-done.9.other_1_ref
  90.0 0.0 copy-done
  90.0 0.0 copy-done.1
  90.0 0.0 copy-done.2
  90.0 0.0 copy-done.3
  90.0 8.3 %conv_module.1 = (bf16[128,768]{1,0:T(8,128)(2,1)}, bf16[128,768]{1,0:T(8,128)(2,1)}) custom-call(s32[2]{0:T(128)S(1)} %copy-done.5, s32[3]{0:T(128)S(1)} %bitcast.11, bf16[192,384]{1,0:T(8,128)(2,1)S(1)} %get-tuple-element.40.same_0_ref, bf16[192,384]{1,0:T(8,128)(2,1)S(1)} %collective-permute-done.5.same_1_ref, ...), custom_call_target="tpu_custom_call" | custom-call | tf_op jit(solution)/shard_map/conv_module/pallas_call | solution.py:422
  (3 shorter events, 0.0 us)
Async XLA Ops:
  3.3 24.9 %all-to-all-start = ((bf16[64,2,640]{2,1,0:T(2,128)(2,1)}), bf16[64,2,640]{2,1,0:T(2,128)(2,1)S(1)}, u32[]{:S(2)}, u32[]{:S(2)}) async-start(bf16[64,2,640]{2,1,0:T(2,128)(2,1)} %get-tuple-element.28), calls=%async_computation | async-start | bytes 327680 | tf_op jit(solution)/shard_map/all_to_all | solution.py:538
  16.5 19.5 %collective-permute-start = (bf16[152,384]{1,0:T(8,128)(2,1)}, bf16[152,384]{1,0:T(8,128)(2,1)S(1)}, u32[]{:S(2)}, u32[]{:S(2)}) collective-permute-start(bf16[152,384]{1,0:T(8,128)(2,1)} %get-tuple-element.26), channel_id=1, source_target_pairs={{0,0},{1,65},{2,130},{3,195},{4,4},{5,69},{6,134},{7,199},{8,8},{9... | collective-permute-start | bytes 350216 | tf_op jit(solution)/shard_map/ppermute | solution.py:536
  18.0 17.9 %collective-permute-start.1 = (bf16[152,384]{1,0:T(8,128)(2,1)}, bf16[152,384]{1,0:T(8,128)(2,1)S(1)}, u32[]{:S(2)}, u32[]{:S(2)}) collective-permute-start(bf16[152,384]{1,0:T(8,128)(2,1)} %get-tuple-element.27), channel_id=1, source_target_pairs={{0,4},{1,69},{2,134},{3,199},{4,0},{5,65},{6,130},{7,195},{8,12},{... | collective-permute-start | bytes 350216 | tf_op jit(solution)/shard_map/ppermute | solution.py:537
  28.2 0.7 copy-start.7
  31.7 7.2 %collective-permute-start.2 = (bf16[112,256]{1,0:T(8,128)(2,1)}, bf16[112,256]{1,0:T(8,128)(2,1)S(1)}, u32[]{:S(2)}, u32[]{:S(2)}) collective-permute-start(bf16[112,256]{1,0:T(8,128)(2,1)} %get-tuple-element.30), channel_id=1, source_target_pairs={{0,1},{1,2},{2,3},{3,0},{4,5},{5,6},{6,7},{7,4},{8,9},{9,10},{10,1... | collective-permute-start | bytes 172040 | tf_op jit(solution)/shard_map/ppermute | solution.py:551
  33.0 6.0 %collective-permute-start.4 = (bf16[112,256]{1,0:T(8,128)(2,1)}, bf16[112,256]{1,0:T(8,128)(2,1)S(1)}, u32[]{:S(2)}, u32[]{:S(2)}) collective-permute-start(bf16[112,256]{1,0:T(8,128)(2,1)} %get-tuple-element.32), channel_id=1, source_target_pairs={{0,3},{1,0},{2,1},{3,2},{4,7},{5,4},{6,5},{7,6},{8,11},{9,8},{10,9... | collective-permute-start | bytes 172040 | tf_op jit(solution)/shard_map/ppermute | solution.py:551
  34.4 4.5 %collective-permute-start.3 = (bf16[64,256]{1,0:T(8,128)(2,1)}, bf16[64,256]{1,0:T(8,128)(2,1)S(1)}, u32[]{:S(2)}, u32[]{:S(2)}) collective-permute-start(bf16[64,256]{1,0:T(8,128)(2,1)} %get-tuple-element.31), channel_id=1, source_target_pairs={{0,2},{1,3},{2,0},{3,1},{4,6},{5,7},{6,4},{7,5},{8,10},{9,11},{10,... | collective-permute-start | bytes 98312 | tf_op jit(solution)/shard_map/ppermute | solution.py:551
  40.3 4.7 %copy-start.8 = (bf16[9,512]{1,0:T(8,128)(2,1)S(1)}, bf16[9,512]{1,0:T(8,128)(2,1)}, u32[]{:S(2)}) copy-start(bf16[9,512]{1,0:T(8,128)(2,1)} %param.16) | copy-start | bytes 27652
  40.3 4.7 %copy-start.4 = (bf16[64,256]{1,0:T(8,128)(2,1)S(1)}, bf16[64,256]{1,0:T(8,128)(2,1)}, u32[]{:S(2)}) copy-start(bf16[64,256]{1,0:T(8,128)(2,1)} %get-tuple-element.33.refs_0_) | copy-start | bytes 98308
  40.3 4.7 %copy-start.5 = (s32[2]{0:T(128)S(1)}, s32[2]{0:T(128)}, u32[]{:S(2)}) copy-start(s32[2]{0:T(128)} %pad_add_fusion.place_ref) | copy-start | bytes 28
  40.3 4.7 %copy-start.6 = (s32[1,3]{1,0:T(1,128)S(1)}, s32[1,3]{1,0:T(1,128)}, u32[]{:S(2)}) copy-start(s32[1,3]{1,0:T(1,128)} %param.15) | copy-start | bytes 40
  40.3 27.3 %all-to-all-start.1 = ((bf16[8,304,384]{2,1,0:T(8,128)(2,1)}), bf16[8,304,384]{2,1,0:T(8,128)(2,1)}, u32[]{:S(2)}, u32[]{:S(2)}) async-start(bf16[8,304,384]{2,1,0:T(8,128)(2,1)} %broadcast_in_dim.18), calls=%async_computation.1 | async-start | bytes 3735552 | tf_op jit(solution)/shard_map/all_to_all | solution.py:502
  67.6 9.0 %collective-permute-start.8 = (bf16[2432,384]{1,0:T(8,128)(2,1)}, bf16[2432,384]{1,0:T(8,128)(2,1)S(1)}, u32[]{:S(2)}, u32[]{:S(2)}) collective-permute-start(bf16[2432,384]{1,0:T(8,128)(2,1)} %bitcast.5.proj_hbm), channel_id=1, source_target_pairs={{0,4},{4,0},{8,12},{12,8},{16,20},{20,16},{24,28},{28,24},{32,36},... | collective-permute-start | bytes 5603336 | tf_op jit(solution)/shard_map/ppermute | solution.py:558
  72.8 10.1 %collective-permute-start.5 = (bf16[192,384]{1,0:T(8,128)(2,1)S(1)}, bf16[192,384]{1,0:T(8,128)(2,1)S(1)}, u32[]{:S(2)}, u32[]{:S(2)}) collective-permute-start(bf16[192,384]{1,0:T(8,128)(2,1)S(1)} %get-tuple-element.41), channel_id=1, source_target_pairs={{0,1},{1,2},{2,3},{3,0},{4,5},{5,6},{6,7},{7,4},{8,9},{9,10},{10,1... | collective-permute-start | bytes 442376 | tf_op jit(solution)/shard_map/ppermute | solution.py:563
  73.2 9.8 %collective-permute-start.6 = (bf16[192,384]{1,0:T(8,128)(2,1)S(1)}, bf16[192,384]{1,0:T(8,128)(2,1)S(1)}, u32[]{:S(2)}, u32[]{:S(2)}) collective-permute-start(bf16[192,384]{1,0:T(8,128)(2,1)S(1)} %get-tuple-element.42), channel_id=1, source_target_pairs={{0,2},{1,3},{2,0},{3,1},{4,6},{5,7},{6,4},{7,5},{8,10},{9,11},{10,... | collective-permute-start | bytes 442376 | tf_op jit(solution)/shard_map/ppermute | solution.py:563
  75.5 7.6 %copy-start.9 = (f32[768]{0:T(1024)S(1)}, f32[768]{0:T(1024)}, u32[]{:S(2)}) copy-start(f32[768]{0:T(1024)} %param.19) | copy-start | bytes 9220
  75.5 7.6 %copy-start.10 = (f32[768]{0:T(1024)S(1)}, f32[768]{0:T(1024)}, u32[]{:S(2)}) copy-start(f32[768]{0:T(1024)} %param.22) | copy-start | bytes 9220
  75.5 14.6 %copy-start = (bf16[768,1536]{1,0:T(8,128)(2,1)S(1)}, bf16[768,1536]{1,0:T(8,128)(2,1)}, u32[]{:S(2)}) copy-start(bf16[768,1536]{1,0:T(8,128)(2,1)} %point_in_ref.1) | copy-start | bytes 7077892
  75.5 14.6 %copy-start.1 = (bf16[768,768]{1,0:T(8,128)(2,1)S(1)}, bf16[768,768]{1,0:T(8,128)(2,1)}, u32[]{:S(2)}) copy-start(bf16[768,768]{1,0:T(8,128)(2,1)} %point_out_ref.1) | copy-start | bytes 3538948
  75.5 14.6 %copy-start.2 = (bf16[1,128,768]{2,1,0:T(8,128)(2,1)S(1)}, bf16[1,128,768]{2,1,0:T(8,128)(2,1)}, u32[]{:S(2)}) copy-start(bf16[1,128,768]{2,1,0:T(8,128)(2,1)} %param.24) | copy-start | bytes 589828
  75.5 14.5 %copy-start.3 = (f32[31,768]{1,0:T(8,128)S(1)}, f32[31,768]{1,0:T(8,128)}, u32[]{:S(2)}) copy-start(f32[31,768]{1,0:T(8,128)} %taps_ref.1) | copy-start | bytes 285700
  75.5 7.6 %collective-permute-start.7 = (bf16[192,384]{1,0:T(8,128)(2,1)S(1)}, bf16[192,384]{1,0:T(8,128)(2,1)S(1)}, u32[]{:S(2)}, u32[]{:S(2)}) collective-permute-start(bf16[192,384]{1,0:T(8,128)(2,1)S(1)} %get-tuple-element.43), channel_id=1, source_target_pairs={{0,3},{1,0},{2,1},{3,2},{4,7},{5,4},{6,5},{7,6},{8,11},{9,8},{10,9... | collective-permute-start | bytes 442376 | tf_op jit(solution)/shard_map/ppermute | solution.py:563
  80.0 6.1 %collective-permute-start.10 = (bf16[192,384]{1,0:T(8,128)(2,1)S(1)}, bf16[192,384]{1,0:T(8,128)(2,1)S(1)}, u32[]{:S(2)}, u32[]{:S(2)}) collective-permute-start(bf16[192,384]{1,0:T(8,128)(2,1)S(1)} %get-tuple-element.46), channel_id=1, source_target_pairs={{0,2},{1,3},{2,0},{3,1},{4,6},{5,7},{6,4},{7,5},{8,10},{9,11},{10,... | collective-permute-start | bytes 442376 | tf_op jit(solution)/shard_map/ppermute | solution.py:563
  81.6 7.8 %collective-permute-start.11 = (bf16[192,384]{1,0:T(8,128)(2,1)S(1)}, bf16[192,384]{1,0:T(8,128)(2,1)S(1)}, u32[]{:S(2)}, u32[]{:S(2)}) collective-permute-start(bf16[192,384]{1,0:T(8,128)(2,1)S(1)} %get-tuple-element.47), channel_id=1, source_target_pairs={{0,3},{1,0},{2,1},{3,2},{4,7},{5,4},{6,5},{7,6},{8,11},{9,8},{10,9... | collective-permute-start | bytes 442376 | tf_op jit(solution)/shard_map/ppermute | solution.py:563
  83.0 7.1 %collective-permute-start.9 = (bf16[192,384]{1,0:T(8,128)(2,1)S(1)}, bf16[192,384]{1,0:T(8,128)(2,1)S(1)}, u32[]{:S(2)}, u32[]{:S(2)}) collective-permute-start(bf16[192,384]{1,0:T(8,128)(2,1)S(1)} %get-tuple-element.45), channel_id=1, source_target_pairs={{0,1},{1,2},{2,3},{3,0},{4,5},{5,6},{6,7},{7,4},{8,9},{9,10},{10,1... | collective-permute-start | bytes 442376 | tf_op jit(solution)/shard_map/ppermute | solution.py:563

commit v2 on v1

--- a/solution.py
+++ b/solution.py
@@ -245,15 +245,29 @@
     )(place, lengths, *blocks, conv1_weight, conv2_weight)
 
 
-def proj_kernel(place_ref, features_ref, proj_hbm, *refs):
-    out_refs, (result_ref, proj_ref, sems) = refs[:-3], refs[-3:]
+def proj_kernel(place_ref, features_hbm, proj_hbm, *refs):
+    out_refs, refs = refs[:-5], refs[-5:]
+    result_ref, proj_ref, sems, features_ref, feature_sems = refs
     group, seat = place_ref[0], place_ref[1]
-    for part in range(PROJ_PARTS):
-        proj_copy(proj_hbm, proj_ref, sems, part).start()
+    blocks = feature_sems.shape[0]
+    size = features_ref.shape[1] // blocks
+
+    def feature_copy(block):
+        columns = pl.ds(block * size, size)
+        return pltpu.make_async_copy(
+            features_hbm.at[:, columns], features_ref.at[:, columns], feature_sems.at[block]
+        )
+
+    for part in range(blocks):
+        if part < PROJ_PARTS:
+            proj_copy(proj_hbm, proj_ref, sems, part).start()
+        feature_copy(part).start()
     zero_rims(proj_ref, proj_hbm.shape[0])
 
-    def features(column, size):
-        return features_ref[:, column : column + size]
+    def features(column, count):
+        if column % size == 0:
+            feature_copy(column // size).wait()
+        return features_ref[:, column : column + count]
 
     def wait(part):
         proj_copy(proj_hbm, proj_ref, sems, part).wait()
@@ -275,12 +289,14 @@
     return pl.pallas_call(
         proj_kernel,
         out_shape=[shape] * seats,
-        in_specs=[SMEM, VMEM, HBM],
+        in_specs=[SMEM, HBM, HBM],
         out_specs=[VMEM] * seats,
         scratch_shapes=[
             pltpu.VMEM((frames, half), BF16),
             pltpu.VMEM((rows + 256, half), BF16),
             pltpu.SemaphoreType.DMA((PROJ_PARTS,)),
+            pltpu.VMEM(features.shape, BF16),
+            pltpu.SemaphoreType.DMA((BINS,)),
         ],
         compiler_params=pltpu.CompilerParams(vmem_limit_bytes=40 * 1024 * 1024),
         name="projection",
@@ -346,17 +362,24 @@
     cot_ref,
     cot_high_ref,
     gain_in_ref,
-    point_in_ref,
+    point_in_hbm,
     taps_ref,
     gain_mid_ref,
-    point_out_ref,
+    point_out_hbm,
     encoded_ref,
     grad_ref,
     glu_ref,
     seg_ref,
     mixed_ref,
     back_ref,
+    point_in_ref,
+    point_out_ref,
+    sems,
 ):
+    point_in_copy = pltpu.make_async_copy(point_in_hbm, point_in_ref, sems.at[0])
+    point_out_copy = pltpu.make_async_copy(point_out_hbm, point_out_ref, sems.at[1])
+    point_in_copy.start()
+    point_out_copy.start()
     own, width = cot_ref.shape
     total = own + 2 * RIM
     inner = own + RIM
@@ -370,6 +393,7 @@
     encoder = jnp.concatenate(halves, axis=1).astype(BF16).astype(F32)
     normed_in, inv_in = layer_norm(encoder)
     ln_in = (normed_in * gain_in_ref[...]).astype(BF16)
+    point_in_copy.wait()
     left = dot(ln_in, point_in_ref[:, 0:width])
     gate = jax.nn.sigmoid(dot(ln_in, point_in_ref[:, width : 2 * width]))
     glu_out = (left * gate).astype(BF16).astype(F32)
@@ -392,6 +416,7 @@
     logistic = jax.nn.sigmoid(scaled)
     slope = logistic * (1.0 + scaled * (1.0 - logistic))
     low = RIM - skip
+    point_out_copy.wait()
     hidden = (scaled * logistic)[low : low + own].astype(BF16)
     encoded = encoder[RIM : RIM + own] + dot(hidden, point_out_ref[...])
     encoded_ref[...] = encoded.astype(BF16)
@@ -422,13 +447,16 @@
     return pl.pallas_call(
         module_kernel,
         out_shape=(shape, shape),
-        in_specs=[SMEM, SMEM] + [VMEM] * 16,
+        in_specs=[SMEM, SMEM] + [VMEM] * 12 + [HBM, VMEM, VMEM, HBM],
         out_specs=(VMEM, VMEM),
         scratch_shapes=[
             pltpu.VMEM((8, own + 2 * RIM, width), F32),
             pltpu.VMEM((8, own + 2 * RIM, 128), jnp.int32),
             pltpu.VMEM((inner, width), F32),
             pltpu.VMEM((own, width), F32),
+            pltpu.VMEM(point_in.shape, BF16),
+            pltpu.VMEM(point_out.shape, BF16),
+            pltpu.SemaphoreType.DMA((2,)),
         ],
         compiler_params=pltpu.CompilerParams(vmem_limit_bytes=48 * 1024 * 1024),
         name="conv_module",

time: 98.7 us -> 100 us (1.013)
  Pallas kernels: 41.6 us -> 43.1 us
where the time goes in v2:
time: 100 us
  Pallas kernels  43.1 us (43%)
  starting transfers between devices  32.5 us (32%)
  waiting for transfers between devices  20.6 us (21%)
  local copies, waits for them, and re-layouts  2.12 us (2%)
  between operations  1 us (1%)
    pallas_call x1, Pallas kernels, conv_features(): pl.pallas_call(conv_kernel, out_shape=jax.ShapeDtypeStruct((frames, BINS...  19.7 us
    all_to_all x1, starting transfers between devices, local(): lax.all_to_all(outgoing, 'dp', split_axis=0, concat_axis=0, tiled=True)  13.2 us
    pallas_call x1, Pallas kernels, conv_module(): pl.pallas_call(module_kernel, out_shape=(shape, shape), in_specs=[SMEM, S...  9.18 us
    all_to_all x1, waiting for transfers between devices, local(): lax.all_to_all(outgoing, 'dp', split_axis=0, concat_axis=0, tiled=True)  7.93 us
    pallas_call x2, Pallas kernels, projected_parts(): pl.pallas_call(proj_kernel, out_shape=[shape] * seats, in_specs=[SMEM, HB...  7.55 us
    ppermute x6, waiting for transfers between devices, local(): lax.ppermute(sums[step], 'seq', ring(step))  6.94 us
    ppermute x6, starting transfers between devices, local(): lax.ppermute(sums[step], 'seq', ring(step))  6.75 us
    all_to_all x1, starting transfers between devices, gather_share(): lax.all_to_all(copies, 'dp', split_axis=0, concat_axis=0, tiled=True, axi...  4.64 us
  transfers between devices with their start and end apart: 14, of which 6 were waited for; matrix products, arithmetic and copies ran while one was open for 0% of the time, Pallas kernels for 32%

profile of v2, /device:TPU:1, one launch (start us, length us, event | category | flops | bytes accessed | tf_op | source)
XLA Modules:
  0.0 100.1 jit_solution(16383073215968707190)
XLA Ops:
  0.6 0.6 pad_add_fusion.place_ref
  1.2 2.1 %send.1 = (bf16[64,2,640]{2,1,0:T(2,128)(2,1)}, bf16[152,384]{1,0:T(8,128)(2,1)}, bf16[152,384]{1,0:T(8,128)(2,1)}) custom-call(s32[2]{0:T(128)} %pad_add_fusion.place_ref, bf16[64,640]{1,0:T(8,128)(2,1)} %bitcast.12, s32[1,4096]{1,0:T(1,128)} %dest_ref.3, bf16[152,768]{1,0:T(8,128)(2,1)} %proj_ref.1), custom_call_target="tpu_custom_call" | custom-call | tf_op jit(solution)/shard_map/send/pallas_call | solution.py:468
  3.3 13.2 %all-to-all-start = ((bf16[64,2,640]{2,1,0:T(2,128)(2,1)}), bf16[64,2,640]{2,1,0:T(2,128)(2,1)S(1)}, u32[]{:S(2)}, u32[]{:S(2)}) async-start(bf16[64,2,640]{2,1,0:T(2,128)(2,1)} %get-tuple-element.28), calls=%async_computation | async-start | bytes 327680 | tf_op jit(solution)/shard_map/all_to_all | solution.py:566
  16.5 1.6 %collective-permute-start = (bf16[152,384]{1,0:T(8,128)(2,1)}, bf16[152,384]{1,0:T(8,128)(2,1)S(1)}, u32[]{:S(2)}, u32[]{:S(2)}) collective-permute-start(bf16[152,384]{1,0:T(8,128)(2,1)} %get-tuple-element.26), channel_id=1, source_target_pairs={{0,0},{1,65},{2,130},{3,195},{4,4},{5,69},{6,134},{7,199},{8,8},{9... | collective-permute-start | bytes 350216 | tf_op jit(solution)/shard_map/ppermute | solution.py:564
  18.0 0.5 collective-permute-start.1
  18.5 1.7 %landing.1.landing_ref = bf16[2,64,64]{2,1,0:T(8,128)(2,1)} custom-call(s32[2]{0:T(128)} %pad_add_fusion.place_ref, s32[1,4096]{1,0:T(1,128)} %dest_ref.3), custom_call_target="tpu_custom_call" | custom-call | tf_op jit(solution)/shard_map/landing/pallas_call | solution.py:478
  20.2 7.9 %all-to-all-done.arrived_ref = bf16[64,2,640]{2,1,0:T(2,128)(2,1)S(1)} async-done(((bf16[64,2,640]{2,1,0:T(2,128)(2,1)}), bf16[64,2,640]{2,1,0:T(2,128)(2,1)S(1)}, u32[]{:S(2)}, u32[]{:S(2)}) %all-to-all-start) | async-done | bytes 163872 | tf_op jit(solution)/shard_map/all_to_all | solution.py:566
  28.2 0.0 copy-start.7
  28.2 0.7 copy-done.7
  28.8 2.9 %place.1 = (bf16[64,256]{1,0:T(8,128)(2,1)}, bf16[112,256]{1,0:T(8,128)(2,1)}, bf16[64,256]{1,0:T(8,128)(2,1)}, bf16[112,256]{1,0:T(8,128)(2,1)}) custom-call(s32[2]{0:T(128)} %pad_add_fusion.place_ref, bf16[64,2,640]{2,1,0:T(2,128)(2,1)} %copy-done.7, bf16[2,64,64]{2,1,0:T(8,128)(2,1)} %landing.1.landing_ref, bf16[640,1024]{1,0:T(8,128)(2,1)} %constant.27.clone.cut_ref, ...), custom_call_target="tpu_custom_call" | custom-call | tf_op jit(solution)/shard_map/place/pallas_call | solution.py:502
  31.7 1.2 %collective-permute-start.2 = (bf16[112,256]{1,0:T(8,128)(2,1)}, bf16[112,256]{1,0:T(8,128)(2,1)S(1)}, u32[]{:S(2)}, u32[]{:S(2)}) collective-permute-start(bf16[112,256]{1,0:T(8,128)(2,1)} %get-tuple-element.30), channel_id=1, source_target_pairs={{0,1},{1,2},{2,3},{3,0},{4,5},{5,6},{6,7},{7,4},{8,9},{9,10},{10,1... | collective-permute-start | bytes 172040 | tf_op jit(solution)/shard_map/ppermute | solution.py:579
  33.0 1.5 %collective-permute-start.4 = (bf16[112,256]{1,0:T(8,128)(2,1)}, bf16[112,256]{1,0:T(8,128)(2,1)S(1)}, u32[]{:S(2)}, u32[]{:S(2)}) collective-permute-start(bf16[112,256]{1,0:T(8,128)(2,1)} %get-tuple-element.32), channel_id=1, source_target_pairs={{0,3},{1,0},{2,1},{3,2},{4,7},{5,4},{6,5},{7,6},{8,11},{9,8},{10,9... | collective-permute-start | bytes 172040 | tf_op jit(solution)/shard_map/ppermute | solution.py:579
  34.4 1.5 %collective-permute-start.3 = (bf16[64,256]{1,0:T(8,128)(2,1)}, bf16[64,256]{1,0:T(8,128)(2,1)S(1)}, u32[]{:S(2)}, u32[]{:S(2)}) collective-permute-start(bf16[64,256]{1,0:T(8,128)(2,1)} %get-tuple-element.31), channel_id=1, source_target_pairs={{0,2},{1,3},{2,0},{3,1},{4,6},{5,7},{6,4},{7,5},{8,10},{9,11},{10,... | collective-permute-start | bytes 98312 | tf_op jit(solution)/shard_map/ppermute | solution.py:579
  36.0 0.0 collective-permute-done
  36.0 0.0 collective-permute-done.1
  36.0 0.1 maximum_select_fusion
  36.0 2.9 %collective-permute-done.3.refs_2_ = bf16[64,256]{1,0:T(8,128)(2,1)S(1)} collective-permute-done((bf16[64,256]{1,0:T(8,128)(2,1)}, bf16[64,256]{1,0:T(8,128)(2,1)S(1)}, u32[]{:S(2)}, u32[]{:S(2)}) %collective-permute-start.3) | collective-permute-done | bytes 32800 | tf_op jit(solution)/shard_map/ppermute | solution.py:579
  38.9 0.0 collective-permute-done.2.refs_1_.cot_low_ref
  38.9 0.0 collective-permute-done.4.refs_3_.cot_high_ref
  38.9 1.4 %broadcast_in_dim.18 = bf16[8,304,384]{2,1,0:T(8,128)(2,1)} broadcast(bf16[304,384]{1,0:T(8,128)(2,1)S(1)} %maximum_select_fusion), dimensions={1,2} | broadcast | bytes 2101248 | tf_op jit(solution)/shard_map/broadcast_in_dim | solution.py:529
  40.3 0.0 copy-start.8
  40.3 0.0 copy-start.4
  40.3 0.0 copy-start.5
  40.3 0.0 copy-start.6
  40.3 4.6 %all-to-all-start.1 = ((bf16[8,304,384]{2,1,0:T(8,128)(2,1)}), bf16[8,304,384]{2,1,0:T(8,128)(2,1)}, u32[]{:S(2)}, u32[]{:S(2)}) async-start(bf16[8,304,384]{2,1,0:T(8,128)(2,1)} %broadcast_in_dim.18), calls=%async_computation.1 | async-start | bytes 3735552 | tf_op jit(solution)/shard_map/all_to_all | solution.py:530
  45.0 0.0 copy-done.8
  45.0 0.0 copy-done.4
  45.0 0.0 copy-done.5
  45.0 0.0 copy-done.6
  45.0 19.7 %convolutions.1.features_hbm = bf16[512,2560]{1,0:T(8,128)(2,1)S(1)} custom-call(s32[2]{0:T(128)S(1)} %copy-done.5, s32[3]{0:T(128)S(1)} %bitcast.10, bf16[64,256]{1,0:T(8,128)(2,1)S(1)} %copy-done.4, bf16[112,256]{1,0:T(8,128)(2,1)S(1)} %collective-permute-done.2.refs_1_.cot_low_ref, bf16[64,256]{1,0:T(8,128)(2,1)S(1)} %collective-permute-done.3.refs_2_, ...), custom_call_target="tpu_custom_call" | custom-call | tf_op jit(solution)/shard_map/convolutions/pallas_call | solution.py:232
  64.7 2.9 %all-to-all-done.1 = bf16[8,304,384]{2,1,0:T(8,128)(2,1)} async-done(((bf16[8,304,384]{2,1,0:T(8,128)(2,1)}), bf16[8,304,384]{2,1,0:T(8,128)(2,1)}, u32[]{:S(2)}, u32[]{:S(2)}) %all-to-all-start.1) | async-done | bytes 1867808 | tf_op jit(solution)/shard_map/all_to_all | solution.py:530
  67.6 1.7 %collective-permute-start.8 = (bf16[2432,384]{1,0:T(8,128)(2,1)}, bf16[2432,384]{1,0:T(8,128)(2,1)S(1)}, u32[]{:S(2)}, u32[]{:S(2)}) collective-permute-start(bf16[2432,384]{1,0:T(8,128)(2,1)} %bitcast.5.proj_hbm), channel_id=1, source_target_pairs={{0,4},{4,0},{8,12},{12,8},{16,20},{20,16},{24,28},{28,24},{32,36},... | collective-permute-start | bytes 5603336 | tf_op jit(solution)/shard_map/ppermute | solution.py:586
  69.3 3.7 %projection.2 = (bf16[192,384]{1,0:T(8,128)(2,1)S(1)}, bf16[192,384]{1,0:T(8,128)(2,1)S(1)}, bf16[192,384]{1,0:T(8,128)(2,1)S(1)}, bf16[192,384]{1,0:T(8,128)(2,1)S(1)}) custom-call(s32[2]{0:T(128)S(1)} %copy-done.5, bf16[512,2560]{1,0:T(8,128)(2,1)S(1)} %convolutions.1.features_hbm, bf16[2432,384]{1,0:T(8,128)(2,1)} %bitcast.5.proj_hbm), custom_call_target="tpu_custom_call" | custom-call | tf_op jit(solution)/shard_map/projection/pallas_call | solution.py:289
  73.1 0.4 collective-permute-start.5
  73.5 2.2 %collective-permute-start.6 = (bf16[192,384]{1,0:T(8,128)(2,1)S(1)}, bf16[192,384]{1,0:T(8,128)(2,1)S(1)}, u32[]{:S(2)}, u32[]{:S(2)}) collective-permute-start(bf16[192,384]{1,0:T(8,128)(2,1)S(1)} %get-tuple-element.42), channel_id=1, source_target_pairs={{0,2},{1,3},{2,0},{3,1},{4,6},{5,7},{6,4},{7,5},{8,10},{9,11},{10,... | collective-permute-start | bytes 442376 | tf_op jit(solution)/shard_map/ppermute | solution.py:591
  75.7 0.0 copy-start.9
  75.7 0.0 copy-start.10
  75.7 0.0 copy-start
  75.7 0.0 copy-start.1
  75.7 0.0 copy-start.2
  75.7 0.0 copy-start.3
  75.7 1.1 %collective-permute-start.7 = (bf16[192,384]{1,0:T(8,128)(2,1)S(1)}, bf16[192,384]{1,0:T(8,128)(2,1)S(1)}, u32[]{:S(2)}, u32[]{:S(2)}) collective-permute-start(bf16[192,384]{1,0:T(8,128)(2,1)S(1)} %get-tuple-element.43), channel_id=1, source_target_pairs={{0,3},{1,0},{2,1},{3,2},{4,7},{5,4},{6,5},{7,6},{8,11},{9,8},{10,9... | collective-permute-start | bytes 442376 | tf_op jit(solution)/shard_map/ppermute | solution.py:591
  76.9 0.0 collective-permute-done.8.proj_hbm
  76.9 3.8 %projection.3 = (bf16[192,384]{1,0:T(8,128)(2,1)S(1)}, bf16[192,384]{1,0:T(8,128)(2,1)S(1)}, bf16[192,384]{1,0:T(8,128)(2,1)S(1)}, bf16[192,384]{1,0:T(8,128)(2,1)S(1)}) custom-call(s32[2]{0:T(128)S(1)} %copy-done.5, bf16[512,2560]{1,0:T(8,128)(2,1)S(1)} %convolutions.1.features_hbm, bf16[2432,384]{1,0:T(8,128)(2,1)S(1)} %collective-permute-done.8.proj_hbm), custom_call_target="tpu_custom_call" | custom-call | tf_op jit(solution)/shard_map/projection/pallas_call | solution.py:289
  80.7 1.5 %collective-permute-start.10 = (bf16[192,384]{1,0:T(8,128)(2,1)S(1)}, bf16[192,384]{1,0:T(8,128)(2,1)S(1)}, u32[]{:S(2)}, u32[]{:S(2)}) collective-permute-start(bf16[192,384]{1,0:T(8,128)(2,1)S(1)} %get-tuple-element.46), channel_id=1, source_target_pairs={{0,2},{1,3},{2,0},{3,1},{4,6},{5,7},{6,4},{7,5},{8,10},{9,11},{10,... | collective-permute-start | bytes 442376 | tf_op jit(solution)/shard_map/ppermute | solution.py:591
  82.2 1.4 %collective-permute-start.11 = (bf16[192,384]{1,0:T(8,128)(2,1)S(1)}, bf16[192,384]{1,0:T(8,128)(2,1)S(1)}, u32[]{:S(2)}, u32[]{:S(2)}) collective-permute-start(bf16[192,384]{1,0:T(8,128)(2,1)S(1)} %get-tuple-element.47), channel_id=1, source_target_pairs={{0,3},{1,0},{2,1},{3,2},{4,7},{5,4},{6,5},{7,6},{8,11},{9,8},{10,9... | collective-permute-start | bytes 442376 | tf_op jit(solution)/shard_map/ppermute | solution.py:591
  83.6 0.0 collective-permute-done.5.same_1_ref
  83.6 0.1 collective-permute-start.9
  83.7 0.0 copy-done.9
  83.7 0.0 copy-done.10
  83.7 0.0 collective-permute-done.6.same_2_ref
  83.7 0.0 collective-permute-done.7.same_3_ref
  83.7 3.1 %collective-permute-done.10.other_2_ref = bf16[192,384]{1,0:T(8,128)(2,1)S(1)} collective-permute-done((bf16[192,384]{1,0:T(8,128)(2,1)S(1)}, bf16[192,384]{1,0:T(8,128)(2,1)S(1)}, u32[]{:S(2)}, u32[]{:S(2)}) %collective-permute-start.10) | collective-permute-done | bytes 147488 | tf_op jit(solution)/shard_map/ppermute | solution.py:591
  86.8 2.8 %collective-permute-done.11.other_3_ref = bf16[192,384]{1,0:T(8,128)(2,1)S(1)} collective-permute-done((bf16[192,384]{1,0:T(8,128)(2,1)S(1)}, bf16[192,384]{1,0:T(8,128)(2,1)S(1)}, u32[]{:S(2)}, u32[]{:S(2)}) %collective-permute-start.11) | collective-permute-done | bytes 147488 | tf_op jit(solution)/shard_map/ppermute | solution.py:591
  89.6 1.1 %collective-permute-done.9.other_1_ref = bf16[192,384]{1,0:T(8,128)(2,1)S(1)} collective-permute-done((bf16[192,384]{1,0:T(8,128)(2,1)S(1)}, bf16[192,384]{1,0:T(8,128)(2,1)S(1)}, u32[]{:S(2)}, u32[]{:S(2)}) %collective-permute-start.9) | collective-permute-done | bytes 147488 | tf_op jit(solution)/shard_map/ppermute | solution.py:591
  90.7 0.0 copy-done
  90.7 0.0 copy-done.1
  90.7 0.0 copy-done.2
  90.7 0.0 copy-done.3
  90.7 9.2 %conv_module.1 = (bf16[128,768]{1,0:T(8,128)(2,1)}, bf16[128,768]{1,0:T(8,128)(2,1)}) custom-call(s32[2]{0:T(128)S(1)} %copy-done.5, s32[3]{0:T(128)S(1)} %bitcast.11, bf16[192,384]{1,0:T(8,128)(2,1)S(1)} %get-tuple-element.40.same_0_ref, bf16[192,384]{1,0:T(8,128)(2,1)S(1)} %collective-permute-done.5.same_1_ref, ...), custom_call_target="tpu_custom_call" | custom-call | tf_op jit(solution)/shard_map/conv_module/pallas_call | solution.py:447
  (3 shorter events, 0.0 us)
Async XLA Ops:
  3.3 24.9 %all-to-all-start = ((bf16[64,2,640]{2,1,0:T(2,128)(2,1)}), bf16[64,2,640]{2,1,0:T(2,128)(2,1)S(1)}, u32[]{:S(2)}, u32[]{:S(2)}) async-start(bf16[64,2,640]{2,1,0:T(2,128)(2,1)} %get-tuple-element.28), calls=%async_computation | async-start | bytes 327680 | tf_op jit(solution)/shard_map/all_to_all | solution.py:566
  16.5 19.5 %collective-permute-start = (bf16[152,384]{1,0:T(8,128)(2,1)}, bf16[152,384]{1,0:T(8,128)(2,1)S(1)}, u32[]{:S(2)}, u32[]{:S(2)}) collective-permute-start(bf16[152,384]{1,0:T(8,128)(2,1)} %get-tuple-element.26), channel_id=1, source_target_pairs={{0,0},{1,65},{2,130},{3,195},{4,4},{5,69},{6,134},{7,199},{8,8},{9... | collective-permute-start | bytes 350216 | tf_op jit(solution)/shard_map/ppermute | solution.py:564
  18.0 17.9 %collective-permute-start.1 = (bf16[152,384]{1,0:T(8,128)(2,1)}, bf16[152,384]{1,0:T(8,128)(2,1)S(1)}, u32[]{:S(2)}, u32[]{:S(2)}) collective-permute-start(bf16[152,384]{1,0:T(8,128)(2,1)} %get-tuple-element.27), channel_id=1, source_target_pairs={{0,4},{1,69},{2,134},{3,199},{4,0},{5,65},{6,130},{7,195},{8,12},{... | collective-permute-start | bytes 350216 | tf_op jit(solution)/shard_map/ppermute | solution.py:565
  28.2 0.7 copy-start.7
  31.7 7.2 %collective-permute-start.2 = (bf16[112,256]{1,0:T(8,128)(2,1)}, bf16[112,256]{1,0:T(8,128)(2,1)S(1)}, u32[]{:S(2)}, u32[]{:S(2)}) collective-permute-start(bf16[112,256]{1,0:T(8,128)(2,1)} %get-tuple-element.30), channel_id=1, source_target_pairs={{0,1},{1,2},{2,3},{3,0},{4,5},{5,6},{6,7},{7,4},{8,9},{9,10},{10,1... | collective-permute-start | bytes 172040 | tf_op jit(solution)/shard_map/ppermute | solution.py:579
  33.0 6.0 %collective-permute-start.4 = (bf16[112,256]{1,0:T(8,128)(2,1)}, bf16[112,256]{1,0:T(8,128)(2,1)S(1)}, u32[]{:S(2)}, u32[]{:S(2)}) collective-permute-start(bf16[112,256]{1,0:T(8,128)(2,1)} %get-tuple-element.32), channel_id=1, source_target_pairs={{0,3},{1,0},{2,1},{3,2},{4,7},{5,4},{6,5},{7,6},{8,11},{9,8},{10,9... | collective-permute-start | bytes 172040 | tf_op jit(solution)/shard_map/ppermute | solution.py:579
  34.4 4.5 %collective-permute-start.3 = (bf16[64,256]{1,0:T(8,128)(2,1)}, bf16[64,256]{1,0:T(8,128)(2,1)S(1)}, u32[]{:S(2)}, u32[]{:S(2)}) collective-permute-start(bf16[64,256]{1,0:T(8,128)(2,1)} %get-tuple-element.31), channel_id=1, source_target_pairs={{0,2},{1,3},{2,0},{3,1},{4,6},{5,7},{6,4},{7,5},{8,10},{9,11},{10,... | collective-permute-start | bytes 98312 | tf_op jit(solution)/shard_map/ppermute | solution.py:579
  40.3 4.7 %copy-start.8 = (bf16[9,512]{1,0:T(8,128)(2,1)S(1)}, bf16[9,512]{1,0:T(8,128)(2,1)}, u32[]{:S(2)}) copy-start(bf16[9,512]{1,0:T(8,128)(2,1)} %param.16) | copy-start | bytes 27652
  40.3 4.7 %copy-start.4 = (bf16[64,256]{1,0:T(8,128)(2,1)S(1)}, bf16[64,256]{1,0:T(8,128)(2,1)}, u32[]{:S(2)}) copy-start(bf16[64,256]{1,0:T(8,128)(2,1)} %get-tuple-element.33.refs_0_) | copy-start | bytes 98308
  40.3 4.7 %copy-start.5 = (s32[2]{0:T(128)S(1)}, s32[2]{0:T(128)}, u32[]{:S(2)}) copy-start(s32[2]{0:T(128)} %pad_add_fusion.place_ref) | copy-start | bytes 28
  40.3 4.7 %copy-start.6 = (s32[1,3]{1,0:T(1,128)S(1)}, s32[1,3]{1,0:T(1,128)}, u32[]{:S(2)}) copy-start(s32[1,3]{1,0:T(1,128)} %param.15) | copy-start | bytes 40
  40.3 27.3 %all-to-all-start.1 = ((bf16[8,304,384]{2,1,0:T(8,128)(2,1)}), bf16[8,304,384]{2,1,0:T(8,128)(2,1)}, u32[]{:S(2)}, u32[]{:S(2)}) async-start(bf16[8,304,384]{2,1,0:T(8,128)(2,1)} %broadcast_in_dim.18), calls=%async_computation.1 | async-start | bytes 3735552 | tf_op jit(solution)/shard_map/all_to_all | solution.py:530
  67.6 9.3 %collective-permute-start.8 = (bf16[2432,384]{1,0:T(8,128)(2,1)}, bf16[2432,384]{1,0:T(8,128)(2,1)S(1)}, u32[]{:S(2)}, u32[]{:S(2)}) collective-permute-start(bf16[2432,384]{1,0:T(8,128)(2,1)} %bitcast.5.proj_hbm), channel_id=1, source_target_pairs={{0,4},{4,0},{8,12},{12,8},{16,20},{20,16},{24,28},{28,24},{32,36},... | collective-permute-start | bytes 5603336 | tf_op jit(solution)/shard_map/ppermute | solution.py:586
  73.1 10.5 %collective-permute-start.5 = (bf16[192,384]{1,0:T(8,128)(2,1)S(1)}, bf16[192,384]{1,0:T(8,128)(2,1)S(1)}, u32[]{:S(2)}, u32[]{:S(2)}) collective-permute-start(bf16[192,384]{1,0:T(8,128)(2,1)S(1)} %get-tuple-element.41), channel_id=1, source_target_pairs={{0,1},{1,2},{2,3},{3,0},{4,5},{5,6},{6,7},{7,4},{8,9},{9,10},{10,1... | collective-permute-start | bytes 442376 | tf_op jit(solution)/shard_map/ppermute | solution.py:591
  73.5 10.2 %collective-permute-start.6 = (bf16[192,384]{1,0:T(8,128)(2,1)S(1)}, bf16[192,384]{1,0:T(8,128)(2,1)S(1)}, u32[]{:S(2)}, u32[]{:S(2)}) collective-permute-start(bf16[192,384]{1,0:T(8,128)(2,1)S(1)} %get-tuple-element.42), channel_id=1, source_target_pairs={{0,2},{1,3},{2,0},{3,1},{4,6},{5,7},{6,4},{7,5},{8,10},{9,11},{10,... | collective-permute-start | bytes 442376 | tf_op jit(solution)/shard_map/ppermute | solution.py:591
  75.7 8.0 %copy-start.9 = (f32[768]{0:T(1024)S(1)}, f32[768]{0:T(1024)}, u32[]{:S(2)}) copy-start(f32[768]{0:T(1024)} %param.19) | copy-start | bytes 9220
  75.7 8.0 %copy-start.10 = (f32[768]{0:T(1024)S(1)}, f32[768]{0:T(1024)}, u32[]{:S(2)}) copy-start(f32[768]{0:T(1024)} %param.22) | copy-start | bytes 9220
  75.7 15.0 %copy-start = (bf16[768,1536]{1,0:T(8,128)(2,1)S(1)}, bf16[768,1536]{1,0:T(8,128)(2,1)}, u32[]{:S(2)}) copy-start(bf16[768,1536]{1,0:T(8,128)(2,1)} %point_in_hbm.1) | copy-start | bytes 7077892
  75.7 15.0 %copy-start.1 = (bf16[768,768]{1,0:T(8,128)(2,1)S(1)}, bf16[768,768]{1,0:T(8,128)(2,1)}, u32[]{:S(2)}) copy-start(bf16[768,768]{1,0:T(8,128)(2,1)} %point_out_hbm.1) | copy-start | bytes 3538948
  75.7 15.0 %copy-start.2 = (bf16[1,128,768]{2,1,0:T(8,128)(2,1)S(1)}, bf16[1,128,768]{2,1,0:T(8,128)(2,1)}, u32[]{:S(2)}) copy-start(bf16[1,128,768]{2,1,0:T(8,128)(2,1)} %param.24) | copy-start | bytes 589828
  75.7 14.9 %copy-start.3 = (f32[31,768]{1,0:T(8,128)S(1)}, f32[31,768]{1,0:T(8,128)}, u32[]{:S(2)}) copy-start(f32[31,768]{1,0:T(8,128)} %taps_ref.1) | copy-start | bytes 285700
  75.7 8.0 %collective-permute-start.7 = (bf16[192,384]{1,0:T(8,128)(2,1)S(1)}, bf16[192,384]{1,0:T(8,128)(2,1)S(1)}, u32[]{:S(2)}, u32[]{:S(2)}) collective-permute-start(bf16[192,384]{1,0:T(8,128)(2,1)S(1)} %get-tuple-element.43), channel_id=1, source_target_pairs={{0,3},{1,0},{2,1},{3,2},{4,7},{5,4},{6,5},{7,6},{8,11},{9,8},{10,9... | collective-permute-start | bytes 442376 | tf_op jit(solution)/shard_map/ppermute | solution.py:591
  80.7 6.1 %collective-permute-start.10 = (bf16[192,384]{1,0:T(8,128)(2,1)S(1)}, bf16[192,384]{1,0:T(8,128)(2,1)S(1)}, u32[]{:S(2)}, u32[]{:S(2)}) collective-permute-start(bf16[192,384]{1,0:T(8,128)(2,1)S(1)} %get-tuple-element.46), channel_id=1, source_target_pairs={{0,2},{1,3},{2,0},{3,1},{4,6},{5,7},{6,4},{7,5},{8,10},{9,11},{10,... | collective-permute-start | bytes 442376 | tf_op jit(solution)/shard_map/ppermute | solution.py:591
  82.2 7.4 %collective-permute-start.11 = (bf16[192,384]{1,0:T(8,128)(2,1)S(1)}, bf16[192,384]{1,0:T(8,128)(2,1)S(1)}, u32[]{:S(2)}, u32[]{:S(2)}) collective-permute-start(bf16[192,384]{1,0:T(8,128)(2,1)S(1)} %get-tuple-element.47), channel_id=1, source_target_pairs={{0,3},{1,0},{2,1},{3,2},{4,7},{5,4},{6,5},{7,6},{8,11},{9,8},{10,9... | collective-permute-start | bytes 442376 | tf_op jit(solution)/shard_map/ppermute | solution.py:591
  83.6 7.1 %collective-permute-start.9 = (bf16[192,384]{1,0:T(8,128)(2,1)S(1)}, bf16[192,384]{1,0:T(8,128)(2,1)S(1)}, u32[]{:S(2)}, u32[]{:S(2)}) collective-permute-start(bf16[192,384]{1,0:T(8,128)(2,1)S(1)} %get-tuple-element.45), channel_id=1, source_target_pairs={{0,1},{1,2},{2,3},{3,0},{4,5},{5,6},{6,7},{7,4},{8,9},{9,10},{10,1... | collective-permute-start | bytes 442376 | tf_op jit(solution)/shard_map/ppermute | solution.py:591
